TPU v7x, 32 devices: a whole 2x2x4 slice. The times are simulated.
32 devices in a mesh: ctx: 16 (over z, y, x), head: 2 (over core).
Axes of the slice: x: 2, y: 2, z: 4, core: 2. Of those that a mesh axis runs over, the one named last changes fastest.
Arguments:
- lin_q: bfloat16 [8192, 8, 128], P('ctx', 'head'), may hold values from -1.5 to 1.5
- lin_k: bfloat16 [8192, 8, 128], P('ctx', 'head'), may hold values from -1.5 to 1.5
- lin_v: bfloat16 [8192, 8, 128], P('ctx', 'head'), may hold values from -3 to 3
- lin_dout: bfloat16 [8192, 8, 128], P('ctx', 'head'), may hold values from -0.29882812 to 0.29882812
- lin_decay: float32 [8, 8192], P('head', 'ctx'), may hold values from -1 to 0
- att_q: bfloat16 [8192, 8, 128], P('ctx', 'head'), may hold values from -64 to 64
- att_k: bfloat16 [8192, 128], P('ctx'), may hold values from -6 to 6
- att_v: bfloat16 [8192, 128], P('ctx'), may hold values from -6 to 6
- att_dout: bfloat16 [8192, 8, 128], P('ctx', 'head'), may hold values from -1.796875 to 1.796875
- doc_block: int32 [32], replicated, may hold values from 0 to 4, as said below
Outputs:
- lin_dq: bfloat16 [8192, 8, 128], P('ctx', 'head')
- lin_dk: bfloat16 [8192, 8, 128], P('ctx', 'head')
- lin_dv: bfloat16 [8192, 8, 128], P('ctx', 'head')
- att_dq: bfloat16 [8192, 8, 128], P('ctx', 'head')
- att_dk: bfloat16 [8192, 128], P(('ctx', 'head'))
- att_dv: bfloat16 [8192, 128], P(('ctx', 'head'))
Inputs may be any that keep to these rules, and one draw needn't show every extreme that they name: doc_block starts at 0, never falls and rises by at most one from block to block; each document spans 1 to 12 blocks; the first spans exactly 12.
All inputs are finite; a program needn't handle non-finite values.
Results may differ from a plain program's by a relative error of at most 0.0052.
Values may be sent and summed in bfloat16 or wider, within the bound.
A program may use at most 128 MiB of HBM per device.

v0:
```python
import functools
import math

import jax
import jax.numpy as jnp
from jax import lax
from jax.experimental import pallas as pl
from jax.experimental.pallas import tpu as pltpu
from jax.sharding import PartitionSpec as P

TILE = 256
MOST = 12
NEG = -1e30
MESH = pl.DeviceIdType.MESH
F32 = jnp.float32
BF16 = jnp.bfloat16
SHAPE = jax.ShapeDtypeStruct
DMA = pltpu.SemaphoreType.DMA
IN_VMEM = pl.BlockSpec(memory_space=pltpu.VMEM)
IN_SMEM = pl.BlockSpec(memory_space=pltpu.SMEM)
ANYWHERE = pl.BlockSpec(memory_space=pl.ANY)
VMEM_LIMIT = 56 * 1024 * 1024


def dot_nn(a, b):
    return lax.dot_general(a, b, (((1,), (0,)), ((), ())), preferred_element_type=F32)


def dot_nt(a, b):
    return lax.dot_general(a, b, (((1,), (1,)), ((), ())), preferred_element_type=F32)


def dot_tn(a, b):
    return lax.dot_general(a, b, (((0,), (0,)), ((), ())), preferred_element_type=F32)


def split(x):
    high = x.astype(BF16)
    return high, (x - high.astype(F32)).astype(BF16)


def greet(me, core, count, reach):
    barrier = pltpu.get_barrier_semaphore()
    pl.semaphore_signal(barrier, inc=1, device_id={"head": 1 - core}, device_id_type=MESH)
    for step in range(1, reach + 1):

        @pl.when(me + step < count)
        def _():
            pl.semaphore_signal(barrier, inc=1, device_id={"ctx": me + step}, device_id_type=MESH)

        @pl.when(me - step >= 0)
        def _():
            pl.semaphore_signal(barrier, inc=1, device_id={"ctx": me - step}, device_id_type=MESH)

    pl.semaphore_wait(
        barrier, 1 + jnp.minimum(me, reach) + jnp.minimum(count - 1 - me, reach)
    )


def decay_terms(me, count, nblocks, doc, dec):
    t_sub = lax.broadcasted_iota(jnp.int32, (TILE, TILE), 0)
    t_lane = lax.broadcasted_iota(jnp.int32, (TILE, TILE), 1)
    upper = (t_sub <= t_lane).astype(F32)
    lower = (t_sub >= t_lane).astype(F32)

    def link(at_one, at_two):
        one = jnp.clip(at_one, 0, count * nblocks - 1)
        two = jnp.clip(at_two, 0, count * nblocks - 1)
        inside = jnp.logical_and(at_one >= 0, at_two < count * nblocks)
        same = jnp.logical_and(doc[one] == doc[two], inside)
        return jnp.where(same, 1.0, 0.0).astype(F32)

    follows = [link(me * nblocks + b - 1, me * nblocks + b) for b in range(nblocks)]
    precedes = [link(me * nblocks + b, me * nblocks + b + 1) for b in range(nblocks)]

    cum_row, cum_col = [], []
    for b in range(nblocks):
        piece = dec[:, b * TILE : (b + 1) * TILE]
        cum_row.append(
            lax.dot_general(
                piece, upper, (((1,), (0,)), ((), ())),
                preferred_element_type=F32, precision=lax.Precision.HIGHEST,
            )
        )
        cum_col.append(
            lax.dot_general(
                lower, piece, (((1,), (1,)), ((), ())),
                preferred_element_type=F32, precision=lax.Precision.HIGHEST,
            )
        )

    def head_terms(b, h):
        row = cum_row[b][h : h + 1, :]
        col = cum_col[b][:, h : h + 1]
        total = col[TILE - 1 : TILE, :]
        return row, col, total

    return follows, precedes, head_terms, t_sub, t_lane


def lightning_kernel(
    count, reach, heads, nblocks,
    doc, lq, lk, lv, ld, dec_in, att_k, att_v,
    send_l, send_r, parts, states, kall, vall,
    wide, raw, dec, raw_sem, own_sem, kv_send, kv_recv, pair_send, pair_recv,
):
    me = lax.axis_index("ctx")
    core = lax.axis_index("head")
    length = nblocks * TILE
    half = length // 2
    width = lq.shape[1]
    rows = TILE * heads
    loads = [
        pltpu.make_async_copy(ref, raw.at[a], raw_sem.at[a])
        for a, ref in enumerate((lq, lk, lv, ld))
    ]
    loads.append(pltpu.make_async_copy(dec_in, dec, raw_sem.at[4]))
    for load in loads:
        load.start()
    greet(me, core, count, reach)

    pairs = ((att_k, kall), (att_v, vall))
    start = pl.multiple_of(core * half, half)

    def kv_copy(which, step):
        source, target = pairs[which]
        place = pl.multiple_of((reach - step) * length + core * half, half)
        return pltpu.make_async_remote_copy(
            src_ref=source.at[pl.ds(start, half)],
            dst_ref=target.at[pl.ds(place, half)],
            send_sem=kv_send.at[which, step - 1],
            recv_sem=kv_recv.at[which, step - 1],
            device_id={"ctx": me + step},
            device_id_type=MESH,
        )

    def pair_copy(which, step):
        target = pairs[which][1]
        place = pl.multiple_of((reach - step) * length + core * half, half)
        return pltpu.make_async_remote_copy(
            src_ref=target.at[pl.ds(place, half)],
            dst_ref=target.at[pl.ds(place, half)],
            send_sem=pair_send.at[which, step - 1],
            recv_sem=pair_recv.at[which, step - 1],
            device_id={"head": 1 - core},
            device_id_type=MESH,
        )

    for step in range(1, reach + 1):

        @pl.when(me + step < count)
        def _():
            kv_copy(0, step).start()
            kv_copy(1, step).start()

    own = [
        pltpu.make_async_copy(
            pairs[which][0], pairs[which][1].at[pl.ds(reach * length, length)], own_sem.at[which]
        )
        for which in range(2)
    ]
    own[0].start()
    own[1].start()

    for load in loads:
        load.wait()
    follows, precedes, head_terms, _, _ = decay_terms(me, count, nblocks, doc, dec)

    for b in range(nblocks):
        for a in range(4):
            wide[a] = raw[a, b * rows : (b + 1) * rows, :].astype(F32)
        for h in range(heads):
            row, col, total = head_terms(b, h)
            picked = [wide[a, pl.ds(h, TILE, stride=heads), :] for a in range(4)]
            for a in range(4):
                parts[a, b, h] = picked[a].astype(BF16)
            key_high, key_low = split((picked[1] * jnp.exp(total - col)).T)
            value = picked[2].astype(BF16)
            states[0, b, h] = dot_nn(key_high, value) + dot_nn(key_low, value)
            query_high, query_low = split((picked[0] * jnp.exp(col)).T)
            dout = picked[3].astype(BF16)
            states[1, b, h] = dot_nn(query_high, dout) + dot_nn(query_low, dout)

    for h in range(heads):
        keep = [jnp.exp(head_terms(b, h)[2]) for b in range(nblocks)]
        total_l = states[0, 0, h]
        mult_l = keep[0] * follows[0]
        for b in range(1, nblocks):
            total_l = states[0, b, h] + keep[b] * follows[b] * total_l
            mult_l = mult_l * keep[b] * follows[b]
        total_r = states[1, nblocks - 1, h]
        mult_r = keep[nblocks - 1] * precedes[nblocks - 1]
        for b in reversed(range(nblocks - 1)):
            total_r = states[1, b, h] + keep[b] * precedes[b] * total_r
            mult_r = mult_r * keep[b] * precedes[b]
        for send, total, mult in ((send_l, total_l, mult_l), (send_r, total_r, mult_r)):
            high, low = split(jnp.broadcast_to(mult, (16, width)))
            send[h, 0:width, :] = total.astype(BF16)
            send[h, width : width + 16, :] = high
            send[h, width + 16 : width + 32, :] = low

    def pass_on(step):
        @pl.when(me - step >= 0)
        def _():
            for which in range(2):
                kv_copy(which, step).wait_recv()
                pair_copy(which, step).start()

    for step in range(1, reach + 1):
        pass_on(step)
    for step in range(1, reach + 1):

        @pl.when(me - step >= 0)
        def _():
            for which in range(2):
                pair_copy(which, step).wait()

        @pl.when(me + step < count)
        def _():
            for which in range(2):
                kv_copy(which, step).wait_send()

    own[0].wait()
    own[1].wait()


def attention_kernel(
    nblocks, reach, heads, chunk, spot,
    q, dout, keys_in, values, dq, dkey, dvalue, scores, probs_grad, flipped,
):
    index = pl.program_id(0)
    width = q.shape[1]
    scale = width ** (-0.5)
    log2e = math.log2(math.e)
    factor = scale * log2e
    total_blocks = keys_in.shape[0] // TILE

    @pl.when(index == 0)
    def _():
        dkey[...] = jnp.zeros(dkey.shape, F32)
        dvalue[...] = jnp.zeros(dvalue.shape, F32)

        @pl.loop(0, total_blocks)
        def _(j):
            at = pl.ds(pl.multiple_of(j * TILE, TILE), TILE)
            flipped[j] = keys_in[at, :].astype(F32).T.astype(BF16)

    per_block = TILE * heads // chunk
    block = index // per_block
    diag = reach * nblocks + block
    first = diag + 1 - spot[block]
    queries = q[...]
    douts = dout[...]

    token = (lax.broadcasted_iota(jnp.int32, (TILE, chunk), 1) + (index % per_block) * chunk) // heads
    seen = lax.broadcasted_iota(jnp.int32, (TILE, chunk), 0) <= token

    def rows_of(j):
        return pl.ds(pl.multiple_of(j * TILE, TILE), TILE)

    def folded(x, op):
        return op(x.reshape(TILE // 8, 8, chunk), axis=0)

    s = jnp.where(seen, dot_nt(keys_in[rows_of(diag), :], queries), NEG)
    scores[diag] = s

    def find_max(j, top):
        s = dot_nt(keys_in[rows_of(j), :], queries)
        scores[j] = s
        return jnp.maximum(top, folded(s, jnp.max))

    top = lax.fori_loop(first, diag, find_max, folded(s, jnp.max))
    top = jnp.max(top, axis=0, keepdims=True) * factor

    def sums(j, carried):
        amount, weighted = carried
        p = jnp.exp2(scores[j] * factor - top)
        g = dot_nt(values[rows_of(j), :], douts)
        scores[j] = p
        probs_grad[j] = g
        return amount + folded(p, jnp.sum), weighted + folded(p * g, jnp.sum)

    zero = jnp.zeros((8, chunk), F32)
    amount, weighted = lax.fori_loop(first, diag + 1, sums, (zero, zero))
    inverse = 1.0 / jnp.sum(amount, axis=0, keepdims=True)
    delta = jnp.sum(weighted, axis=0, keepdims=True) * inverse

    def grads(j, acc):
        p = scores[j] * inverse
        g = p * (probs_grad[j] - delta)
        p = p.astype(BF16)
        g = g.astype(BF16)
        at = rows_of(j)
        dvalue[at, :] += dot_nn(p, douts)
        dkey[at, :] += dot_nn(g, queries)
        return acc + dot_nn(flipped[j], g)

    acc = lax.fori_loop(first, diag + 1, grads, jnp.zeros((width, chunk), F32))
    dq[...] = (acc.T * scale).astype(BF16)


def reduce_kernel(
    count, reach, heads, nblocks,
    doc, dec, parts, states, got_l1, got_l2, got_l3, got_r1, got_r2, got_r3, dkey, dvalue,
    dq, dk, dv, att_dk, att_dv,
    grads, near, echo, land, paired, out, inbox,
    pair_send, pair_recv, send_sem, recv_sem, echo_send, echo_recv,
):
    me = lax.axis_index("ctx")
    core = lax.axis_index("head")
    length = nblocks * TILE
    half = length // 2
    rows = TILE * heads
    width = dkey.shape[1]
    scale = dkey.shape[1] ** (-0.5)
    greet(me, core, count, reach)
    sources = (dkey, dvalue)

    def pair_copy(which, step):
        place = pl.multiple_of((reach - step) * length + (1 - core) * half, half)
        return pltpu.make_async_remote_copy(
            src_ref=sources[which].at[pl.ds(place, half)],
            dst_ref=paired.at[which, step],
            send_sem=pair_send.at[which, step],
            recv_sem=pair_recv.at[which, step],
            device_id={"head": 1 - core},
            device_id_type=MESH,
        )

    def home_copy(step):
        return pltpu.make_async_remote_copy(
            src_ref=out.at[step - 1],
            dst_ref=inbox.at[step - 1],
            send_sem=send_sem.at[step - 1],
            recv_sem=recv_sem.at[step - 1],
            device_id={"ctx": me - step},
            device_id_type=MESH,
        )

    order = list(range(reach, -1, -1))
    for step in order:
        pair_copy(0, step).start()
        pair_copy(1, step).start()

    follows, precedes, head_terms, t_sub, t_lane = decay_terms(me, count, nblocks, doc, dec)

    def echo_copy(side):
        return pltpu.make_async_remote_copy(
            src_ref=echo.at[side],
            dst_ref=land.at[side],
            send_sem=echo_send.at[side],
            recv_sem=echo_recv.at[side],
            device_id={"ctx": me + 3 if side == 0 else me - 3},
            device_id_type=MESH,
        )

    spans = ([], [])
    for side, got in enumerate(((got_l1, got_l2, got_l3), (got_r1, got_r2, got_r3))):
        for h in range(heads):
            mult = [
                ref[h, width : width + 16, :].astype(F32)[0:1]
                + ref[h, width + 16 : width + 32, :].astype(F32)[0:1]
                for ref in got
            ]
            one, two, three = (ref[h, 0:width, :].astype(F32) for ref in got)
            total = one + mult[0] * (two + mult[1] * three)
            near[side, h] = total
            echo[side, h] = total.astype(BF16)
            spans[side].append(mult[0] * mult[1] * mult[2])

    before = (me - 3 >= 0, me + 3 < count)
    after = (me + 3 < count, me - 3 >= 0)
    for side in range(2):

        @pl.when(after[side])
        def _():
            echo_copy(side).start()

        @pl.when(jnp.logical_not(before[side]))
        def _():
            land[side] = jnp.zeros(land.shape[1:], BF16)

    def within(b):
        for h in range(heads):
            row, col, total = head_terms(b, h)
            query, key, value, dout = (parts[a, b, h] for a in range(4))
            seen = t_sub <= t_lane
            weight = jnp.where(seen, jnp.exp(jnp.where(seen, row - col, 0.0)), 0.0)
            left = (dot_nt(value, dout) * weight).astype(BF16)
            right = (dot_nt(key, query) * weight).astype(BF16)
            at = pl.ds(b * rows + h, TILE, stride=heads)
            grads[0, at, :] = dot_tn(left, key)
            grads[1, at, :] = dot_nn(left, query)
            grads[2, at, :] = dot_nn(right, dout)

    within(0)

    def mine(which, step):
        place = pl.multiple_of((reach - step) * length + core * half, half)
        return sources[which][pl.ds(place, half), :] + paired[which, step]

    for step in order:
        for which in range(2):
            pair_copy(which, step).wait_recv()
        if step > 0:
            for which in range(2):
                out[step - 1, which] = mine(which, step).astype(BF16)

            @pl.when(me - step >= 0)
            def _():
                home_copy(step).start()

        if step > 0:

            @pl.when(me + step >= count)
            def _():
                inbox[step - 1] = jnp.zeros(inbox.shape[1:], BF16)

    for b in range(1, nblocks):
        within(b)
    for side in range(2):

        @pl.when(before[side])
        def _():
            echo_copy(side).wait_recv()

    for h in range(heads):
        keep = [jnp.exp(head_terms(b, h)[2]) for b in range(nblocks)]
        state = near[0, h] + spans[0][h] * land[0, h].astype(F32)
        into = []
        for b in range(nblocks):
            into.append(follows[b] * state)
            state = states[0, b, h] + keep[b] * into[b]
        state = near[1, h] + spans[1][h] * land[1, h].astype(F32)
        back = [None] * nblocks
        for b in reversed(range(nblocks)):
            back[b] = precedes[b] * state
            state = states[1, b, h] + keep[b] * back[b]
        for b in range(nblocks):
            row, col, total = head_terms(b, h)
            query, key, value, dout = (parts[a, b, h] for a in range(4))
            head_decay = jnp.exp(col)
            tail_decay = jnp.exp(total - col)
            into_high, into_low = split(into[b])
            back_high, back_low = split(back[b])
            at = pl.ds(b * rows + h, TILE, stride=heads)
            grads[0, at, :] = grads[0, at, :] + head_decay * (
                dot_nt(dout, into_high) + dot_nt(dout, into_low)
            )
            grads[1, at, :] = grads[1, at, :] + tail_decay * (
                dot_nt(value, back_high) + dot_nt(value, back_low)
            )
            grads[2, at, :] = grads[2, at, :] + tail_decay * (
                dot_nn(key, back_high) + dot_nn(key, back_low)
            )
    dq[...] = grads[0].astype(BF16)
    dk[...] = grads[1].astype(BF16)
    dv[...] = grads[2].astype(BF16)

    paired[0, 0] = mine(0, 0)
    paired[1, 0] = mine(1, 0)
    for step in range(1, reach + 1):

        @pl.when(me + step < count)
        def _():
            home_copy(step).wait_recv()

        for which in range(2):
            paired[which, 0] += inbox[step - 1, which].astype(F32)
    att_dk[...] = (paired[0, 0] * scale).astype(BF16)
    att_dv[...] = paired[1, 0].astype(BF16)
    for step in order:
        pair_copy(0, step).wait_send()
        pair_copy(1, step).wait_send()
        if step > 0:

            @pl.when(me - step >= 0)
            def _():
                home_copy(step).wait_send()
    for side in range(2):

        @pl.when(after[side])
        def _():
            echo_copy(side).wait_send()


def call_lightning(count, lin_q, lin_k, lin_v, lin_dout, lin_decay, att_k, att_v, doc_block):
    length, heads, width = lin_q.shape
    nblocks = length // TILE
    reach = -(-(MOST - 1) // nblocks)
    rows = length * heads
    window = (reach + 1) * length
    state = (heads, width, width)
    flat = lambda x: x.reshape(rows, width)
    return pl.pallas_call(
        functools.partial(lightning_kernel, count, reach, heads, nblocks),
        out_shape=[
            SHAPE((heads, width + 32, width), BF16),
            SHAPE((heads, width + 32, width), BF16),
            SHAPE((4, nblocks, heads, TILE, width), BF16),
            SHAPE((2, nblocks) + state, F32),
            SHAPE((window, width), BF16),
            SHAPE((window, width), BF16),
        ],
        in_specs=[IN_SMEM] + [ANYWHERE] * 7,
        out_specs=[IN_VMEM] * 4 + [ANYWHERE] * 2,
        scratch_shapes=[
            pltpu.VMEM((4, TILE * heads, width), F32),
            pltpu.VMEM((4, rows, width), BF16),
            pltpu.VMEM(lin_decay.shape, F32),
            DMA((5,)),
            DMA((2,)),
            DMA((2, reach)),
            DMA((2, reach)),
            DMA((2, reach)),
            DMA((2, reach)),
        ],
        compiler_params=pltpu.CompilerParams(
            collective_id=0, has_side_effects=True, vmem_limit_bytes=VMEM_LIMIT
        ),
        name="lightning",
    )(doc_block, flat(lin_q), flat(lin_k), flat(lin_v), flat(lin_dout), lin_decay, att_k, att_v)


def call_attention(chunk, spot, att_q, att_dout, kall, vall):
    length, heads, width = att_q.shape
    nblocks = length // TILE
    rows = length * heads
    window = kall.shape[0]
    reach = window // length - 1
    flat = lambda x: x.reshape(rows, width)
    return pl.pallas_call(
        functools.partial(attention_kernel, nblocks, reach, heads, chunk),
        grid_spec=pltpu.PrefetchScalarGridSpec(
            num_scalar_prefetch=1,
            grid=(rows // chunk,),
            in_specs=[
                pl.BlockSpec((chunk, width), lambda i, s: (i, 0)),
                pl.BlockSpec((chunk, width), lambda i, s: (i, 0)),
                pl.BlockSpec((window, width), lambda i, s: (0, 0)),
                pl.BlockSpec((window, width), lambda i, s: (0, 0)),
            ],
            out_specs=[
                pl.BlockSpec((chunk, width), lambda i, s: (i, 0)),
                pl.BlockSpec((window, width), lambda i, s: (0, 0)),
                pl.BlockSpec((window, width), lambda i, s: (0, 0)),
            ],
            scratch_shapes=[
                pltpu.VMEM((window // TILE, TILE, chunk), F32),
                pltpu.VMEM((window // TILE, TILE, chunk), F32),
                pltpu.VMEM((window // TILE, width, TILE), BF16),
            ],
        ),
        out_shape=[
            SHAPE((rows, width), BF16),
            SHAPE((window, width), F32),
            SHAPE((window, width), F32),
        ],
        compiler_params=pltpu.CompilerParams(vmem_limit_bytes=50 * 1024 * 1024),
        cost_estimate=pl.CostEstimate(
            flops=10 * width * rows * window, bytes_accessed=8 * window * width, transcendentals=0
        ),
        name="attention",
    )(spot, flat(att_q), flat(att_dout), kall, vall)


def shards(count, lin_q, lin_k, lin_v, lin_dout, lin_decay, att_q, att_k, att_v, att_dout, doc_block):
    length, heads, width = lin_q.shape
    nblocks = length // TILE
    reach = -(-(MOST - 1) // nblocks)
    half = length // 2
    rows = length * heads
    window = (reach + 1) * length
    send_l, send_r, parts, states, kall, vall = call_lightning(
        count, lin_q, lin_k, lin_v, lin_dout, lin_decay, att_k, att_v, doc_block
    )
    got = [
        lax.ppermute(send_l, "ctx", [(i, i + step) for i in range(count - step)])
        for step in (1, 2, 3)
    ] + [
        lax.ppermute(send_r, "ctx", [(i + step, i) for i in range(count - step)])
        for step in (1, 2, 3)
    ]
    me = lax.axis_index("ctx")
    here = lax.dynamic_slice_in_dim(doc_block, me * nblocks, nblocks)
    at = me * nblocks + jnp.arange(nblocks, dtype=jnp.int32)
    before = jnp.sum((doc_block[None, :] < here[:, None]).astype(jnp.int32), axis=1)
    spot = at - before + 1
    att_dq, dkey, dvalue = call_attention(1024, spot, att_q, att_dout, kall, vall)
    lin_dq, lin_dk, lin_dv, att_dk, att_dv = pl.pallas_call(
        functools.partial(reduce_kernel, count, reach, heads, nblocks),
        out_shape=[SHAPE((rows, width), BF16)] * 3 + [SHAPE((half, width), BF16)] * 2,
        in_specs=[IN_SMEM] + [IN_VMEM] * 11,
        out_specs=[IN_VMEM] * 5,
        scratch_shapes=[
            pltpu.VMEM((3, rows, width), F32),
            pltpu.VMEM((2, heads, width, width), F32),
            pltpu.VMEM((2, heads, width, width), BF16),
            pltpu.VMEM((2, heads, width, width), BF16),
            pltpu.VMEM((2, reach + 1, half, width), F32),
            pltpu.VMEM((reach, 2, half, width), BF16),
            pltpu.VMEM((reach, 2, half, width), BF16),
            DMA((2, reach + 1)),
            DMA((2, reach + 1)),
            DMA((reach,)),
            DMA((reach,)),
            DMA((2,)),
            DMA((2,)),
        ],
        compiler_params=pltpu.CompilerParams(
            collective_id=1, has_side_effects=True, vmem_limit_bytes=40 * 1024 * 1024
        ),
        name="reduce",
    )(doc_block, lin_decay, parts, states, *got, dkey, dvalue)
    full = lambda x: x.reshape(length, heads, width)
    return (full(lin_dq), full(lin_dk), full(lin_dv), full(att_dq), att_dk, att_dv)


def solution(mesh):
    return jax.shard_map(
        functools.partial(shards, mesh.shape["ctx"]),
        mesh=mesh,
        in_specs=(
            P("ctx", "head", None),
            P("ctx", "head", None),
            P("ctx", "head", None),
            P("ctx", "head", None),
            P("head", "ctx"),
            P("ctx", "head", None),
            P("ctx", None),
            P("ctx", None),
            P("ctx", "head", None),
            P(),
        ),
        out_specs=(
            P("ctx", "head", None),
            P("ctx", "head", None),
            P("ctx", "head", None),
            P("ctx", "head", None),
            P(("ctx", "head"), None),
            P(("ctx", "head"), None),
        ),
        check_vma=False,
    )
```

profile of v0, /device:TPU:6, one launch (start us, length us, event | category | flops | bytes accessed | tf_op | source)
XLA Modules:
  0.0 115.2 jit_solution(7278445209447544199)
XLA Ops:
  0.6 0.0 copy-start.5
  0.6 0.0 copy-start.8
  0.7 0.0 copy-start.9
  0.7 22.9 %lightning.1 = (bf16[4,160,128]{2,1,0:T(8,128)(2,1)}, bf16[4,160,128]{2,1,0:T(8,128)(2,1)}, bf16[4,2,4,256,128]{4,3,2,1,0:T(8,128)(2,1)}, f32[2,2,4,128,128]{4,3...) custom-call(s32[32]{0:T(128)} %doc.3, bf16[2048,128]{1,0:T(8,128)(2,1)} %bitcast.15, ...), custom_call_target="tpu_custom_call" | custom-call | tf_op jit(solution)/shard_map/lightning/pallas_call | solution.py:495
  23.5 1.9 %collective-permute-start = (bf16[4,160,128]{2,1,0:T(8,128)(2,1)}, bf16[4,160,128]{2,1,0:T(8,128)(2,1)S(1)}, u32[]{:S(2)}, u32[]{:S(2)}) collective-permute-start(bf16[4,160,128]{2,1,0:T(8,128)(2,1)} %get-tuple-element.22), channel_id=1, source_target_pairs={{0,2},{2,4},{4,6},{6,8},{8,10},{10,12},{12,14},{14,16},{16,18},{18... | collective-permute-start | bytes 491528 | tf_op jit(solution)/shard_map/ppermute | solution.py:578
  25.5 4.9 %collective-permute-start.1 = (bf16[4,160,128]{2,1,0:T(8,128)(2,1)}, bf16[4,160,128]{2,1,0:T(8,128)(2,1)S(1)}, u32[]{:S(2)}, u32[]{:S(2)}) collective-permute-start(bf16[4,160,128]{2,1,0:T(8,128)(2,1)} %get-tuple-element.22), channel_id=1, source_target_pairs={{0,4},{2,6},{4,8},{6,10},{8,12},{10,14},{12,16},{14,18},{16,20},{1... | collective-permute-start | bytes 491528 | tf_op jit(solution)/shard_map/ppermute | solution.py:578
  30.4 7.5 %collective-permute-start.2 = (bf16[4,160,128]{2,1,0:T(8,128)(2,1)}, bf16[4,160,128]{2,1,0:T(8,128)(2,1)S(1)}, u32[]{:S(2)}, u32[]{:S(2)}) collective-permute-start(bf16[4,160,128]{2,1,0:T(8,128)(2,1)} %get-tuple-element.22), channel_id=1, source_target_pairs={{0,6},{2,8},{4,10},{6,12},{8,14},{10,16},{12,18},{14,20},{16,22},{... | collective-permute-start | bytes 491528 | tf_op jit(solution)/shard_map/ppermute | solution.py:578
  37.9 3.4 %collective-permute-start.3 = (bf16[4,160,128]{2,1,0:T(8,128)(2,1)}, bf16[4,160,128]{2,1,0:T(8,128)(2,1)S(1)}, u32[]{:S(2)}, u32[]{:S(2)}) collective-permute-start(bf16[4,160,128]{2,1,0:T(8,128)(2,1)} %get-tuple-element.23), channel_id=1, source_target_pairs={{2,0},{4,2},{6,4},{8,6},{10,8},{12,10},{14,12},{16,14},{18,16},{20... | collective-permute-start | bytes 491528 | tf_op jit(solution)/shard_map/ppermute | solution.py:581
  41.3 2.5 %collective-permute-start.4 = (bf16[4,160,128]{2,1,0:T(8,128)(2,1)}, bf16[4,160,128]{2,1,0:T(8,128)(2,1)S(1)}, u32[]{:S(2)}, u32[]{:S(2)}) collective-permute-start(bf16[4,160,128]{2,1,0:T(8,128)(2,1)} %get-tuple-element.23), channel_id=1, source_target_pairs={{4,0},{6,2},{8,4},{10,6},{12,8},{14,10},{16,12},{18,14},{20,16},{2... | collective-permute-start | bytes 491528 | tf_op jit(solution)/shard_map/ppermute | solution.py:581
  43.8 0.0 copy-done.5
  43.8 0.1 dynamic_slice.3
  43.9 0.2 fusion
  44.0 0.0 collective-permute-done.got_l1
  44.1 1.9 %collective-permute-start.5 = (bf16[4,160,128]{2,1,0:T(8,128)(2,1)}, bf16[4,160,128]{2,1,0:T(8,128)(2,1)S(1)}, u32[]{:S(2)}, u32[]{:S(2)}) collective-permute-start(bf16[4,160,128]{2,1,0:T(8,128)(2,1)} %get-tuple-element.23), channel_id=1, source_target_pairs={{6,0},{8,2},{10,4},{12,6},{14,8},{16,10},{18,12},{20,14},{22,16},{... | collective-permute-start | bytes 491528 | tf_op jit(solution)/shard_map/ppermute | solution.py:581
  46.0 0.0 copy-done.8
  46.0 0.0 copy-done.9
  46.0 1.2 %copy-done.6 = bf16[3584,128]{1,0:T(8,128)(2,1)S(1)} copy-done((bf16[3584,128]{1,0:T(8,128)(2,1)S(1)}, bf16[3584,128]{1,0:T(8,128)(2,1)}, u32[]{:S(2)}) %copy-start.6) | copy-done | bytes 917528
  47.2 1.2 %copy-done.7 = bf16[3584,128]{1,0:T(8,128)(2,1)S(1)} copy-done((bf16[3584,128]{1,0:T(8,128)(2,1)S(1)}, bf16[3584,128]{1,0:T(8,128)(2,1)}, u32[]{:S(2)}) %copy-start.7) | copy-done | bytes 917528
  48.4 22.8 %attention.1 = (bf16[2048,128]{1,0:T(8,128)(2,1)}, f32[3584,128]{1,0:T(8,128)}, f32[3584,128]{1,0:T(8,128)}) custom-call(s32[2]{0:T(128)S(1)} %subtract_add_fusion.spot, bf16[2048,128]{1,0:T(8,128)(2,1)S(1)} %bitcast.13, bf16[2048,128]{1,0:T(8,128)(2,1)S(1)} %bitcast.14, bf16[3584,128]{1,0:T(8,128)(2,1)S(1)} %copy-done.6, bf16[3584,128]{1,0:T(8,128)(2,1)S(1)} %copy-done.7), custom_call_target="tpu_custom_call" | custom-call | flops 9395240960 | bytes 3670016 | tf_op jit(solution)/shard_map/attention/pallas_call | solution.py:532
  71.1 0.0 collective-permute-done.1.got_l2
  71.1 0.0 collective-permute-done.2.got_l3
  71.1 0.0 collective-permute-done.3.got_r1
  71.1 0.0 collective-permute-done.4.got_r2
  71.1 0.0 collective-permute-done.5.got_r3
  71.2 1.5 %copy-done.1 = f32[3584,128]{1,0:T(8,128)S(1)} copy-done((f32[3584,128]{1,0:T(8,128)S(1)}, f32[3584,128]{1,0:T(8,128)}, u32[]{:S(2)}) %copy-start.1) | copy-done | bytes 1835032
  72.7 1.5 %copy-done.2 = f32[3584,128]{1,0:T(8,128)S(1)} copy-done((f32[3584,128]{1,0:T(8,128)S(1)}, f32[3584,128]{1,0:T(8,128)}, u32[]{:S(2)}) %copy-start.2) | copy-done | bytes 1835032
  74.2 37.4 %reduce.1 = (bf16[2048,128]{1,0:T(8,128)(2,1)S(1)}, bf16[2048,128]{1,0:T(8,128)(2,1)S(1)}, bf16[2048,128]{1,0:T(8,128)(2,1)S(1)}, bf16[256,128]{1,0:T(8,128)(2,1)S(1)}, bf16[256,128]{1,0:T(8,128)(2,1)S(1)}) custom-call(s32[32]{0:T(128)S(1)} %copy-done.5, f32[4,512]{1,0:T(4,128)S(1)} %copy-done.4, bf16[4,2,4,256,128]{4,3,2,1,0:T(8,128)(2,1)S(1)} %copy-done, ...), custom_call_target="tpu_custom_call" | custom-call | tf_op jit(solution)/shard_map/reduce/pallas_call | solution.py:590
  111.6 0.8 copy.21
  112.4 0.8 copy.22
  113.2 0.8 copy.23
  114.0 0.6 copy.24
  114.6 0.6 copy.25
  (11 shorter events, 0.0 us)
Async XLA Ops:
  0.6 43.1 %copy-start.5 = (s32[32]{0:T(128)S(1)}, s32[32]{0:T(128)}, u32[]{:S(2)}) copy-start(s32[32]{0:T(128)} %doc.3) | copy-start | bytes 388
  0.6 45.3 %copy-start.8 = (bf16[512,4,128]{2,1,0:T(4,128)(2,1)S(1)}, bf16[512,4,128]{2,1,0:T(4,128)(2,1)}, u32[]{:S(2)}) copy-start(bf16[512,4,128]{2,1,0:T(4,128)(2,1)} %param.15) | copy-start | bytes 1572868
  0.7 45.3 %copy-start.9 = (bf16[512,4,128]{2,1,0:T(4,128)(2,1)S(1)}, bf16[512,4,128]{2,1,0:T(4,128)(2,1)}, u32[]{:S(2)}) copy-start(bf16[512,4,128]{2,1,0:T(4,128)(2,1)} %param.18) | copy-start | bytes 1572868
  23.5 20.5 %collective-permute-start = (bf16[4,160,128]{2,1,0:T(8,128)(2,1)}, bf16[4,160,128]{2,1,0:T(8,128)(2,1)S(1)}, u32[]{:S(2)}, u32[]{:S(2)}) collective-permute-start(bf16[4,160,128]{2,1,0:T(8,128)(2,1)} %get-tuple-element.22), channel_id=1, source_target_pairs={{0,2},{2,4},{4,6},{6,8},{8,10},{10,12},{12,14},{14,16},{16,18},{18... | collective-permute-start | bytes 491528 | tf_op jit(solution)/shard_map/ppermute | solution.py:578
  25.5 45.7 %collective-permute-start.1 = (bf16[4,160,128]{2,1,0:T(8,128)(2,1)}, bf16[4,160,128]{2,1,0:T(8,128)(2,1)S(1)}, u32[]{:S(2)}, u32[]{:S(2)}) collective-permute-start(bf16[4,160,128]{2,1,0:T(8,128)(2,1)} %get-tuple-element.22), channel_id=1, source_target_pairs={{0,4},{2,6},{4,8},{6,10},{8,12},{10,14},{12,16},{14,18},{16,20},{1... | collective-permute-start | bytes 491528 | tf_op jit(solution)/shard_map/ppermute | solution.py:578
  30.4 40.8 %collective-permute-start.2 = (bf16[4,160,128]{2,1,0:T(8,128)(2,1)}, bf16[4,160,128]{2,1,0:T(8,128)(2,1)S(1)}, u32[]{:S(2)}, u32[]{:S(2)}) collective-permute-start(bf16[4,160,128]{2,1,0:T(8,128)(2,1)} %get-tuple-element.22), channel_id=1, source_target_pairs={{0,6},{2,8},{4,10},{6,12},{8,14},{10,16},{12,18},{14,20},{16,22},{... | collective-permute-start | bytes 491528 | tf_op jit(solution)/shard_map/ppermute | solution.py:578
  37.9 33.2 %collective-permute-start.3 = (bf16[4,160,128]{2,1,0:T(8,128)(2,1)}, bf16[4,160,128]{2,1,0:T(8,128)(2,1)S(1)}, u32[]{:S(2)}, u32[]{:S(2)}) collective-permute-start(bf16[4,160,128]{2,1,0:T(8,128)(2,1)} %get-tuple-element.23), channel_id=1, source_target_pairs={{2,0},{4,2},{6,4},{8,6},{10,8},{12,10},{14,12},{16,14},{18,16},{20... | collective-permute-start | bytes 491528 | tf_op jit(solution)/shard_map/ppermute | solution.py:581
  41.3 29.9 %collective-permute-start.4 = (bf16[4,160,128]{2,1,0:T(8,128)(2,1)}, bf16[4,160,128]{2,1,0:T(8,128)(2,1)S(1)}, u32[]{:S(2)}, u32[]{:S(2)}) collective-permute-start(bf16[4,160,128]{2,1,0:T(8,128)(2,1)} %get-tuple-element.23), channel_id=1, source_target_pairs={{4,0},{6,2},{8,4},{10,6},{12,8},{14,10},{16,12},{18,14},{20,16},{2... | collective-permute-start | bytes 491528 | tf_op jit(solution)/shard_map/ppermute | solution.py:581
  44.1 27.1 %collective-permute-start.5 = (bf16[4,160,128]{2,1,0:T(8,128)(2,1)}, bf16[4,160,128]{2,1,0:T(8,128)(2,1)S(1)}, u32[]{:S(2)}, u32[]{:S(2)}) collective-permute-start(bf16[4,160,128]{2,1,0:T(8,128)(2,1)} %get-tuple-element.23), channel_id=1, source_target_pairs={{6,0},{8,2},{10,4},{12,6},{14,8},{16,10},{18,12},{20,14},{22,16},{... | collective-permute-start | bytes 491528 | tf_op jit(solution)/shard_map/ppermute | solution.py:581
  46.0 1.2 %copy-start.6 = (bf16[3584,128]{1,0:T(8,128)(2,1)S(1)}, bf16[3584,128]{1,0:T(8,128)(2,1)}, u32[]{:S(2)}) copy-start(bf16[3584,128]{1,0:T(8,128)(2,1)} %get-tuple-element.24.keys_in) | copy-start | bytes 2752516
  47.2 1.2 %copy-start.7 = (bf16[3584,128]{1,0:T(8,128)(2,1)S(1)}, bf16[3584,128]{1,0:T(8,128)(2,1)}, u32[]{:S(2)}) copy-start(bf16[3584,128]{1,0:T(8,128)(2,1)} %get-tuple-element.25.values) | copy-start | bytes 2752516
  48.4 22.8 %copy-start = (bf16[4,2,4,256,128]{4,3,2,1,0:T(8,128)(2,1)S(1)}, bf16[4,2,4,256,128]{4,3,2,1,0:T(8,128)(2,1)}, u32[]{:S(2)}) copy-start(bf16[4,2,4,256,128]{4,3,2,1,0:T(8,128)(2,1)} %get-tuple-element.20.parts) | copy-start | bytes 6291460
  48.4 22.8 %copy-start.3 = (f32[2,2,4,128,128]{4,3,2,1,0:T(8,128)S(1)}, f32[2,2,4,128,128]{4,3,2,1,0:T(8,128)}, u32[]{:S(2)}) copy-start(f32[2,2,4,128,128]{4,3,2,1,0:T(8,128)} %get-tuple-element.21.states) | copy-start | bytes 3145732
  48.4 22.8 %copy-start.4 = (f32[4,512]{1,0:T(4,128)S(1)}, f32[4,512]{1,0:T(4,128)}, u32[]{:S(2)}) copy-start(f32[4,512]{1,0:T(4,128)} %dec.1) | copy-start | bytes 24580
  71.2 1.5 %copy-start.1 = (f32[3584,128]{1,0:T(8,128)S(1)}, f32[3584,128]{1,0:T(8,128)}, u32[]{:S(2)}) copy-start(f32[3584,128]{1,0:T(8,128)} %get-tuple-element.26.dkey) | copy-start | bytes 5505028
  72.7 1.5 %copy-start.2 = (f32[3584,128]{1,0:T(8,128)S(1)}, f32[3584,128]{1,0:T(8,128)}, u32[]{:S(2)}) copy-start(f32[3584,128]{1,0:T(8,128)} %get-tuple-element.27.dvalue) | copy-start | bytes 5505028
where the time goes:
time: 116 us; the launch traced here: 115 us
  Pallas kernels  83 us (72%)
  starting transfers between devices  22.1 us (19%)
  local copies, waits for them, and re-layouts  9.08 us (8%)
    pallas_call x1, Pallas kernels, shards(): pl.pallas_call(functools.partial(reduce_kernel, count, reach, heads, nblo...  37.4 us
    pallas_call x1, Pallas kernels, call_lightning(): pl.pallas_call(functools.partial(lightning_kernel, count, reach, heads, n...  22.9 us
    pallas_call x1, Pallas kernels, call_attention(): pl.pallas_call(functools.partial(attention_kernel, nblocks, reach, heads,...  22.8 us
    ppermute x3, starting transfers between devices, shards(): lax.ppermute(send_l, 'ctx', [(i, i + step) for i in range(count - step)])  14.3 us
    unnamed x25, local copies, waits for them, and re-layouts  9 us
    ppermute x3, starting transfers between devices, shards(): lax.ppermute(send_r, 'ctx', [(i + step, i) for i in range(count - step)])  7.77 us
  transfers between devices with their start and end apart: 6, of which 0 were waited for; matrix products, arithmetic and copies ran while one was open for 0% of the time, Pallas kernels for 20%

commit v1 on v0

v1 whole, which is shorter than its diff:
```python
import functools
import math

import jax
import jax.numpy as jnp
from jax import lax
from jax.experimental import pallas as pl
from jax.experimental.pallas import tpu as pltpu
from jax.sharding import PartitionSpec as P

TILE = 256
MOST = 12
NEG = -1e30
MESH = pl.DeviceIdType.MESH
F32 = jnp.float32
BF16 = jnp.bfloat16
SHAPE = jax.ShapeDtypeStruct
DMA = pltpu.SemaphoreType.DMA
IN_VMEM = pl.BlockSpec(memory_space=pltpu.VMEM)
IN_SMEM = pl.BlockSpec(memory_space=pltpu.SMEM)
ANYWHERE = pl.BlockSpec(memory_space=pl.ANY)
VMEM_LIMIT = 60 * 1024 * 1024


def dot_nn(a, b):
    return lax.dot_general(a, b, (((1,), (0,)), ((), ())), preferred_element_type=F32)


def dot_nt(a, b):
    return lax.dot_general(a, b, (((1,), (1,)), ((), ())), preferred_element_type=F32)


def dot_tn(a, b):
    return lax.dot_general(a, b, (((0,), (0,)), ((), ())), preferred_element_type=F32)


def split(x):
    high = x.astype(BF16)
    return high, (x - high.astype(F32)).astype(BF16)


def decay_terms(me, count, nblocks, doc, dec):
    t_sub = lax.broadcasted_iota(jnp.int32, (TILE, TILE), 0)
    t_lane = lax.broadcasted_iota(jnp.int32, (TILE, TILE), 1)
    upper = (t_sub <= t_lane).astype(F32)
    lower = (t_sub >= t_lane).astype(F32)

    def link(at_one, at_two):
        one = jnp.clip(at_one, 0, count * nblocks - 1)
        two = jnp.clip(at_two, 0, count * nblocks - 1)
        inside = jnp.logical_and(at_one >= 0, at_two < count * nblocks)
        same = jnp.logical_and(doc[one] == doc[two], inside)
        return jnp.where(same, 1.0, 0.0).astype(F32)

    follows = [link(me * nblocks + b - 1, me * nblocks + b) for b in range(nblocks)]
    precedes = [link(me * nblocks + b, me * nblocks + b + 1) for b in range(nblocks)]

    cum_row, cum_col = [], []
    for b in range(nblocks):
        piece = dec[:, b * TILE : (b + 1) * TILE]
        cum_row.append(
            lax.dot_general(
                piece, upper, (((1,), (0,)), ((), ())),
                preferred_element_type=F32, precision=lax.Precision.HIGHEST,
            )
        )
        cum_col.append(
            lax.dot_general(
                lower, piece, (((1,), (1,)), ((), ())),
                preferred_element_type=F32, precision=lax.Precision.HIGHEST,
            )
        )

    def head_terms(b, h):
        row = cum_row[b][h : h + 1, :]
        col = cum_col[b][:, h : h + 1]
        total = col[TILE - 1 : TILE, :]
        return row, col, total

    return follows, precedes, head_terms, t_sub, t_lane


def whole_kernel(
    count, reach, heads, nblocks,
    doc, lq, lk, lv, ld, dec_in, aq, ado, att_k, att_v,
    lin_dq, lin_dk, lin_dv, att_dq, att_dk, att_dv,
    wide, raw, dec, q, dout, kall, vall, parts, states, grads, mixed,
    scores, probs_grad, flipped, dkey, dvalue,
    snd, got, paired, out, inbox,
    raw_sem, kv_send, kv_recv, pair_send, pair_recv, st_send, st_recv,
    pg_send, pg_recv, home_send, home_recv,
):
    me = lax.axis_index("ctx")
    core = lax.axis_index("head")
    length = nblocks * TILE
    width = lq.shape[1]
    rows = TILE * heads
    first_devs = MOST // nblocks
    in_first = me < first_devs
    nleft = jnp.minimum(jnp.where(in_first, me, me - first_devs), reach)
    nright = jnp.minimum(jnp.where(in_first, first_devs - 1 - me, count - 1 - me), reach)
    scale = width ** (-0.5)
    factor = scale * math.log2(math.e)

    loads = [
        pltpu.make_async_copy(ref, raw.at[a], raw_sem.at[a])
        for a, ref in enumerate((lq, lk, lv, ld))
    ]
    loads.append(pltpu.make_async_copy(dec_in, dec, raw_sem.at[4]))
    loads.append(pltpu.make_async_copy(aq, q, raw_sem.at[5]))
    loads.append(pltpu.make_async_copy(ado, dout, raw_sem.at[6]))
    own_rows = pl.ds(reach * length, length)
    loads.append(pltpu.make_async_copy(att_k, kall.at[own_rows], raw_sem.at[7]))
    loads.append(pltpu.make_async_copy(att_v, vall.at[own_rows], raw_sem.at[8]))
    for load in loads:
        load.start()

    barrier = pltpu.get_barrier_semaphore()
    pl.semaphore_signal(barrier, inc=1, device_id={"head": 1 - core}, device_id_type=MESH)
    for step in range(1, reach + 1):

        @pl.when(step <= nright)
        def _():
            pl.semaphore_signal(barrier, inc=1, device_id={"ctx": me + step}, device_id_type=MESH)

        @pl.when(step <= nleft)
        def _():
            pl.semaphore_signal(barrier, inc=1, device_id={"ctx": me - step}, device_id_type=MESH)

    pl.semaphore_wait(barrier, 1 + nleft + nright)

    pairs = ((att_k, kall), (att_v, vall))

    def span(step):
        if step == reach:
            return pl.multiple_of(TILE + core * (TILE // 2), TILE // 2), TILE // 2
        return pl.multiple_of(core * TILE, TILE), TILE

    def kv_copy(which, step):
        start, size = span(step)
        source, target = pairs[which]
        return pltpu.make_async_remote_copy(
            src_ref=source.at[pl.ds(start, size)],
            dst_ref=target.at[pl.ds((reach - step) * length + start, size)],
            send_sem=kv_send.at[which, step - 1],
            recv_sem=kv_recv.at[which, step - 1],
            device_id={"ctx": me + step},
            device_id_type=MESH,
        )

    def pair_copy(which, step):
        start, size = span(step)
        target = pairs[which][1]
        place = pl.ds((reach - step) * length + start, size)
        return pltpu.make_async_remote_copy(
            src_ref=target.at[place],
            dst_ref=target.at[place],
            send_sem=pair_send.at[which, step - 1],
            recv_sem=pair_recv.at[which, step - 1],
            device_id={"head": 1 - core},
            device_id_type=MESH,
        )

    def pass_on(step):
        @pl.when(step <= nleft)
        def _():
            for which in range(2):
                kv_copy(which, step).wait_recv()
                pair_copy(which, step).start()

    def state_copy(side, step):
        return pltpu.make_async_remote_copy(
            src_ref=snd.at[side],
            dst_ref=got.at[side, step - 1],
            send_sem=st_send.at[side, step - 1],
            recv_sem=st_recv.at[side, step - 1],
            device_id={"ctx": me + step if side == 0 else me - step},
            device_id_type=MESH,
        )

    for step in range(1, reach + 1):

        @pl.when(step <= nright)
        def _():
            kv_copy(0, step).start()
            kv_copy(1, step).start()

    for load in loads:
        load.wait()
    follows, precedes, head_terms, t_sub, t_lane = decay_terms(me, count, nblocks, doc, dec)

    for b in range(nblocks):
        for a in range(4):
            wide[a] = raw[a, b * rows : (b + 1) * rows, :].astype(F32)
        for h in range(heads):
            row, col, total = head_terms(b, h)
            picked = [wide[a, pl.ds(h, TILE, stride=heads), :] for a in range(4)]
            for a in range(4):
                parts[a, b, h] = picked[a].astype(BF16)
            key_high, key_low = split((picked[1] * jnp.exp(total - col)).T)
            value = picked[2].astype(BF16)
            states[0, b, h] = dot_nn(key_high, value) + dot_nn(key_low, value)
            query_high, query_low = split((picked[0] * jnp.exp(col)).T)
            dol = picked[3].astype(BF16)
            states[1, b, h] = dot_nn(query_high, dol) + dot_nn(query_low, dol)

    for h in range(heads):
        keep = [jnp.exp(head_terms(b, h)[2]) for b in range(nblocks)]
        total_l = states[0, 0, h]
        mult_l = keep[0] * follows[0]
        for b in range(1, nblocks):
            total_l = states[0, b, h] + keep[b] * follows[b] * total_l
            mult_l = mult_l * keep[b] * follows[b]
        total_r = states[1, nblocks - 1, h]
        mult_r = keep[nblocks - 1] * precedes[nblocks - 1]
        for b in reversed(range(nblocks - 1)):
            total_r = states[1, b, h] + keep[b] * precedes[b] * total_r
            mult_r = mult_r * keep[b] * precedes[b]
        for side, total, mult in ((0, total_l, mult_l), (1, total_r, mult_r)):
            high, low = split(jnp.broadcast_to(mult, (16, width)))
            snd[side, h, 0:width, :] = total.astype(BF16)
            snd[side, h, width : width + 16, :] = high
            snd[side, h, width + 16 : width + 32, :] = low

    pass_on(1)
    pass_on(2)

    def within(b):
        for h in range(heads):
            row, col, total = head_terms(b, h)
            query, key, value, dol = (parts[a, b, h] for a in range(4))
            seen = t_sub <= t_lane
            weight = jnp.where(seen, jnp.exp(jnp.where(seen, row - col, 0.0)), 0.0)
            left = (dot_nt(value, dol) * weight).astype(BF16)
            right = (dot_nt(key, query) * weight).astype(BF16)
            grads[0, b, h] = dot_tn(left, key)
            grads[1, b, h] = dot_nn(left, query)
            grads[2, b, h] = dot_nn(right, dol)

    within(0)
    pass_on(3)
    pass_on(4)
    for b in range(1, nblocks):
        within(b)
    pass_on(5)
    pass_on(6)

    for step in range(1, reach + 1):
        for side, there in ((0, nright), (1, nleft)):

            @pl.when(step <= there)
            def _():
                state_copy(side, step).start()

        for side, there in ((0, nleft), (1, nright)):

            @pl.when(step > there)
            def _():
                got[side, step - 1] = jnp.zeros(got.shape[2:], BF16)

    for step in range(1, reach + 1):

        @pl.when(step <= nleft)
        def _():
            for which in range(2):
                pair_copy(which, step).wait_recv()

    def rows_of(j):
        return pl.ds(pl.multiple_of(j * TILE, TILE), TILE)

    sources = (dkey, dvalue)

    def grad_copy(which, step):
        return pltpu.make_async_remote_copy(
            src_ref=sources[which].at[rows_of((reach - step) * nblocks + 1 - core)],
            dst_ref=paired.at[which, step],
            send_sem=pg_send.at[which, step],
            recv_sem=pg_recv.at[which, step],
            device_id={"head": 1 - core},
            device_id_type=MESH,
        )

    def home_copy(step):
        return pltpu.make_async_remote_copy(
            src_ref=out.at[step - 1],
            dst_ref=inbox.at[step - 1],
            send_sem=home_send.at[step - 1],
            recv_sem=home_recv.at[step - 1],
            device_id={"ctx": me - step},
            device_id_type=MESH,
        )

    def mine(which, step):
        place = rows_of((reach - step) * nblocks + core)
        return sources[which][place, :] + paired[which, step]

    def send_home(step):
        for which in range(2):
            grad_copy(which, step).wait_recv()
        for which in range(2):
            out[step - 1, which] = mine(which, step).astype(BF16)
        home_copy(step).start()

    chunk = rows
    base = reach * nblocks
    dkey[rows_of(base + 1), :] = jnp.zeros((TILE, width), F32)
    dvalue[rows_of(base + 1), :] = jnp.zeros((TILE, width), F32)
    token = lax.broadcasted_iota(jnp.int32, (TILE, chunk), 1) // heads
    seen_q = lax.broadcasted_iota(jnp.int32, (TILE, chunk), 0) <= token

    def folded(x, op):
        return op(x.reshape(TILE // 8, 8, chunk), axis=0)

    def attend(b):
        diag = base + b
        first = jnp.maximum(b + 1, base - nblocks * nleft)
        queries = q[b * chunk : (b + 1) * chunk, :]
        douts = dout[b * chunk : (b + 1) * chunk, :]
        here = doc[me * nblocks + b]

        def hidden(j):
            at = jnp.clip(me * nblocks - base + j, 0, count * nblocks - 1)
            return jnp.where(doc[at] == here, 0.0, -NEG).astype(F32)

        def flip(j):
            flipped[j] = kall[rows_of(j), :].astype(F32).T.astype(BF16)

        s = jnp.where(seen_q, dot_nt(kall[rows_of(diag), :], queries), NEG)
        scores[diag - b - 1] = s
        flip(diag)

        def find_max(j, top):
            s = dot_nt(kall[rows_of(j), :], queries)
            scores[j - b - 1] = s
            if b == 0:
                flip(j)
            return jnp.maximum(top, folded(s, jnp.max) - hidden(j))

        top = lax.fori_loop(first, diag, find_max, folded(s, jnp.max))
        top = jnp.max(top, axis=0, keepdims=True) * factor

        def sums(j, carried):
            amount, weighted = carried
            p = jnp.exp2(scores[j - b - 1] * factor - (top + hidden(j)))
            g = dot_nt(vall[rows_of(j), :], douts)
            scores[j - b - 1] = p
            probs_grad[j - b - 1] = g
            return amount + folded(p, jnp.sum), weighted + folded(p * g, jnp.sum)

        zero = jnp.zeros((8, chunk), F32)
        amount, weighted = lax.fori_loop(first, diag + 1, sums, (zero, zero))
        inverse = 1.0 / jnp.sum(amount, axis=0, keepdims=True)
        delta = jnp.sum(weighted, axis=0, keepdims=True) * inverse

        def one(j, acc):
            p = scores[j - b - 1] * inverse
            g = p * (probs_grad[j - b - 1] - delta)
            p = p.astype(BF16)
            g = g.astype(BF16)
            at = rows_of(j)
            if b == 0:
                dvalue[at, :] = dot_nn(p, douts)
                dkey[at, :] = dot_nn(g, queries)
            else:
                dvalue[at, :] += dot_nn(p, douts)
                dkey[at, :] += dot_nn(g, queries)
            return acc + dot_nn(flipped[j], g)

        acc = jnp.zeros((width, chunk), F32)
        if b == 0:
            acc = lax.fori_loop(first, diag + 1, one, acc)
        else:
            last = jnp.minimum(nleft, reach - 1)

            def by_step(i, acc):
                step = last - i
                j = (reach - step) * nblocks
                acc = one(j + 1, one(j, acc))
                for which in range(2):
                    grad_copy(which, step).start()

                @pl.when(i > 0)
                def _():
                    send_home(step + 1)

                return acc

            acc = lax.fori_loop(0, last + 1, by_step, acc)
        att_dq[b * chunk : (b + 1) * chunk, :] = (acc.T * scale).astype(BF16)

    attend(0)
    far = nleft == reach

    @pl.when(jnp.logical_and(far, core == 0))
    def _():
        for which in range(2):
            grad_copy(which, reach).start()

    @pl.when(jnp.logical_and(far, core == 1))
    def _():
        send_home(reach)

    attend(1)

    for side, there in ((0, nleft), (1, nright)):
        for step in range(1, reach + 1):

            @pl.when(step <= there)
            def _():
                state_copy(side, step).wait_recv()

    for h in range(heads):
        ends = []
        for side in range(2):
            state = jnp.zeros((width, width), F32)
            for step in range(reach, 0, -1):
                mult = (
                    got[side, step - 1, h, width : width + 16, :].astype(F32)[0:1]
                    + got[side, step - 1, h, width + 16 : width + 32, :].astype(F32)[0:1]
                )
                state = got[side, step - 1, h, 0:width, :].astype(F32) + mult * state
            ends.append(state)
        keep = [jnp.exp(head_terms(b, h)[2]) for b in range(nblocks)]
        state = ends[0]
        into = []
        for b in range(nblocks):
            into.append(follows[b] * state)
            state = states[0, b, h] + keep[b] * into[b]
        state = ends[1]
        back = [None] * nblocks
        for b in reversed(range(nblocks)):
            back[b] = precedes[b] * state
            state = states[1, b, h] + keep[b] * back[b]
        for b in range(nblocks):
            row, col, total = head_terms(b, h)
            query, key, value, dol = (parts[a, b, h] for a in range(4))
            head_decay = jnp.exp(col)
            tail_decay = jnp.exp(total - col)
            into_high, into_low = split(into[b])
            back_high, back_low = split(back[b])
            at = pl.ds(b * rows + h, TILE, stride=heads)
            mixed[0, at, :] = grads[0, b, h] + head_decay * (
                dot_nt(dol, into_high) + dot_nt(dol, into_low)
            )
            mixed[1, at, :] = grads[1, b, h] + tail_decay * (
                dot_nt(value, back_high) + dot_nt(value, back_low)
            )
            mixed[2, at, :] = grads[2, b, h] + tail_decay * (
                dot_nn(key, back_high) + dot_nn(key, back_low)
            )
    lin_dq[...] = mixed[0].astype(BF16)
    lin_dk[...] = mixed[1].astype(BF16)
    lin_dv[...] = mixed[2].astype(BF16)

    for which in range(2):
        grad_copy(which, 0).wait_recv()
        paired[which, 0] = mine(which, 0)

    def takes(step, there, who):
        if step < reach:
            return step <= there
        return jnp.logical_and(step <= there, core == who)

    for step in range(1, reach + 1):

        @pl.when(takes(step, nright, 1))
        def _():
            home_copy(step).wait_recv()
            for which in range(2):
                paired[which, 0] += inbox[step - 1, which].astype(F32)

    att_dk[...] = (paired[0, 0] * scale).astype(BF16)
    att_dv[...] = paired[1, 0].astype(BF16)

    for which in range(2):
        grad_copy(which, 0).wait_send()
    for step in range(1, reach + 1):

        @pl.when(step <= nright)
        def _():
            for which in range(2):
                kv_copy(which, step).wait_send()
            state_copy(0, step).wait_send()

        @pl.when(step <= nleft)
        def _():
            for which in range(2):
                pair_copy(which, step).wait_send()
            state_copy(1, step).wait_send()

        @pl.when(takes(step, nleft, 0))
        def _():
            for which in range(2):
                grad_copy(which, step).wait_send()

        @pl.when(takes(step, nleft, 1))
        def _():
            home_copy(step).wait_send()


def shards(count, lin_q, lin_k, lin_v, lin_dout, lin_decay, att_q, att_k, att_v, att_dout, doc_block):
    length, heads, width = lin_q.shape
    nblocks = length // TILE
    assert nblocks == 2
    reach = -(-(MOST - 1) // nblocks)
    rows = length * heads
    window = (reach + 1) * length
    flat = lambda x: x.reshape(rows, width)
    outs = pl.pallas_call(
        functools.partial(whole_kernel, count, reach, heads, nblocks),
        out_shape=[SHAPE((rows, width), BF16)] * 4 + [SHAPE((TILE, width), BF16)] * 2,
        in_specs=[IN_SMEM] + [ANYWHERE] * 9,
        out_specs=[IN_VMEM] * 6,
        scratch_shapes=[
            pltpu.VMEM((4, TILE * heads, width), F32),
            pltpu.VMEM((4, rows, width), BF16),
            pltpu.VMEM(lin_decay.shape, F32),
            pltpu.VMEM((rows, width), BF16),
            pltpu.VMEM((rows, width), BF16),
            pltpu.VMEM((window, width), BF16),
            pltpu.VMEM((window, width), BF16),
            pltpu.VMEM((4, nblocks, heads, TILE, width), BF16),
            pltpu.VMEM((2, nblocks, heads, width, width), F32),
            pltpu.VMEM((3, nblocks, heads, TILE, width), F32),
            pltpu.VMEM((3, rows, width), F32),
            pltpu.VMEM((MOST, TILE, TILE * heads), F32),
            pltpu.VMEM((MOST, TILE, TILE * heads), F32),
            pltpu.VMEM((window // TILE, width, TILE), BF16),
            pltpu.VMEM((window, width), F32),
            pltpu.VMEM((window, width), F32),
            pltpu.VMEM((2, heads, width + 32, width), BF16),
            pltpu.VMEM((2, reach, heads, width + 32, width), BF16),
            pltpu.VMEM((2, reach + 1, TILE, width), F32),
            pltpu.VMEM((reach, 2, TILE, width), BF16),
            pltpu.VMEM((reach, 2, TILE, width), BF16),
            DMA((9,)),
            DMA((2, reach)),
            DMA((2, reach)),
            DMA((2, reach)),
            DMA((2, reach)),
            DMA((2, reach)),
            DMA((2, reach)),
            DMA((2, reach + 1)),
            DMA((2, reach + 1)),
            DMA((reach,)),
            DMA((reach,)),
        ],
        compiler_params=pltpu.CompilerParams(
            collective_id=0, has_side_effects=True, vmem_limit_bytes=VMEM_LIMIT
        ),
        name="whole",
    )(
        doc_block, flat(lin_q), flat(lin_k), flat(lin_v), flat(lin_dout), lin_decay,
        flat(att_q), flat(att_dout), att_k, att_v,
    )
    full = lambda x: x.reshape(length, heads, width)
    return (full(outs[0]), full(outs[1]), full(outs[2]), full(outs[3]), outs[4], outs[5])


def solution(mesh):
    return jax.shard_map(
        functools.partial(shards, mesh.shape["ctx"]),
        mesh=mesh,
        in_specs=(
            P("ctx", "head", None),
            P("ctx", "head", None),
            P("ctx", "head", None),
            P("ctx", "head", None),
            P("head", "ctx"),
            P("ctx", "head", None),
            P("ctx", None),
            P("ctx", None),
            P("ctx", "head", None),
            P(),
        ),
        out_specs=(
            P("ctx", "head", None),
            P("ctx", "head", None),
            P("ctx", "head", None),
            P("ctx", "head", None),
            P(("ctx", "head"), None),
            P(("ctx", "head"), None),
        ),
        check_vma=False,
    )
```

time: 116 us -> 76 us (0.66)
  the two profiles are of different devices: /device:TPU:6 before, /device:TPU:22 now
where the time goes in v1:
time: 76 us; the launch traced here: 75.7 us
  Pallas kernels  68.1 us (90%)
  local copies, waits for them, and re-layouts  6.89 us (9%)
    pallas_call x1, Pallas kernels, shards(): pl.pallas_call(functools.partial(whole_kernel, count, reach, heads, nbloc...  68.1 us
    unnamed x16, local copies, waits for them, and re-layouts  6.89 us

profile of v1, /device:TPU:22, one launch (start us, length us, event | category | flops | bytes accessed | tf_op | source)
XLA Modules:
  0.0 75.7 jit_solution(4941048881443800457)
XLA Ops:
  0.6 68.1 %whole.1 = (bf16[2048,128]{1,0:T(8,128)(2,1)}, bf16[2048,128]{1,0:T(8,128)(2,1)}, bf16[2048,128]{1,0:T(8,128)(2,1)}, bf16[2048,128]{1,0:T(8,128)(2,1)}, bf16[256...) custom-call(s32[32]{0:T(128)} %doc.1, bf16[2048,128]{1,0:T(8,128)(2,1)} %bitcast.14, bf16[2048,128]{1,0:T(8,128)(2,1)} %bitcast.15, ...), custom_call_target="tpu_custom_call" | custom-call | tf_op jit(solution)/shard_map/whole/pallas_call | solution.py:509
  68.8 0.0 copy-start.2
  68.8 2.1 %copy.22 = bf16[512,4,128]{2,1,0:T(4,128)(2,1)} copy(bf16[512,4,128]{2,1,0:T(4,128)(2,1)} %bitcast.13) | data formatting | bytes 1048576
  70.9 0.0 copy-done.2
  70.9 0.0 copy-start.1
  70.9 0.8 %copy.23 = bf16[512,4,128]{2,1,0:T(4,128)(2,1)} copy(bf16[512,4,128]{2,1,0:T(4,128)(2,1)S(1)} %bitcast.12) | data formatting | bytes 1048576
  71.7 0.4 copy-done.1
  72.1 0.0 copy-start
  72.1 0.8 %copy.24 = bf16[512,4,128]{2,1,0:T(4,128)(2,1)} copy(bf16[512,4,128]{2,1,0:T(4,128)(2,1)S(1)} %bitcast.11) | data formatting | bytes 1048576
  72.9 0.4 copy-done
  73.3 0.0 copy-start.4
  73.3 0.8 %copy.25 = bf16[512,4,128]{2,1,0:T(4,128)(2,1)} copy(bf16[512,4,128]{2,1,0:T(4,128)(2,1)S(1)} %bitcast.10) | data formatting | bytes 1048576
  74.1 0.1 copy-done.4
  74.2 0.0 copy-start.3
  74.2 0.6 copy.26
  74.8 0.2 copy-done.3
  75.1 0.6 copy.27
Async XLA Ops:
  68.8 2.1 %copy-start.2 = (bf16[2048,128]{1,0:T(8,128)(2,1)S(1)}, bf16[2048,128]{1,0:T(8,128)(2,1)}, u32[]{:S(2)}) copy-start(bf16[2048,128]{1,0:T(8,128)(2,1)} %get-tuple-element.13) | copy-start | bytes 1572868
  70.9 1.2 %copy-start.1 = (bf16[2048,128]{1,0:T(8,128)(2,1)S(1)}, bf16[2048,128]{1,0:T(8,128)(2,1)}, u32[]{:S(2)}) copy-start(bf16[2048,128]{1,0:T(8,128)(2,1)} %get-tuple-element.14) | copy-start | bytes 1572868
  72.1 1.2 %copy-start = (bf16[2048,128]{1,0:T(8,128)(2,1)S(1)}, bf16[2048,128]{1,0:T(8,128)(2,1)}, u32[]{:S(2)}) copy-start(bf16[2048,128]{1,0:T(8,128)(2,1)} %get-tuple-element.15) | copy-start | bytes 1572868
  73.3 0.9 %copy-start.4 = (bf16[256,128]{1,0:T(8,128)(2,1)S(1)}, bf16[256,128]{1,0:T(8,128)(2,1)}, u32[]{:S(2)}) copy-start(bf16[256,128]{1,0:T(8,128)(2,1)} %get-tuple-element.28) | copy-start | bytes 196612
  74.2 0.9 %copy-start.3 = (bf16[256,128]{1,0:T(8,128)(2,1)S(1)}, bf16[256,128]{1,0:T(8,128)(2,1)}, u32[]{:S(2)}) copy-start(bf16[256,128]{1,0:T(8,128)(2,1)} %get-tuple-element.29) | copy-start | bytes 196612

commit v2 on v1

--- a/solution.py
+++ b/solution.py
@@ -10,6 +10,7 @@
 
 TILE = 256
 MOST = 12
+SHORT = 8
 NEG = -1e30
 MESH = pl.DeviceIdType.MESH
 F32 = jnp.float32
@@ -81,10 +82,10 @@
 
 
 def whole_kernel(
-    count, reach, heads, nblocks,
+    count, limit, heads, nblocks,
     doc, lq, lk, lv, ld, dec_in, aq, ado, att_k, att_v,
     lin_dq, lin_dk, lin_dv, att_dq, att_dk, att_dv,
-    wide, raw, dec, q, dout, kall, vall, parts, states, grads, mixed,
+    wide, raw, dec, q, dout, kall, vall, parts, states, local, grads, mixed,
     scores, probs_grad, flipped, dkey, dvalue,
     snd, got, paired, out, inbox,
     raw_sem, kv_send, kv_recv, pair_send, pair_recv, st_send, st_recv,
@@ -97,8 +98,19 @@
     rows = TILE * heads
     first_devs = MOST // nblocks
     in_first = me < first_devs
-    nleft = jnp.minimum(jnp.where(in_first, me, me - first_devs), reach)
-    nright = jnp.minimum(jnp.where(in_first, first_devs - 1 - me, count - 1 - me), reach)
+    later_reach = limit // nblocks
+    reach = slots_of(limit, nblocks)
+    most = jnp.where(in_first, first_devs - 1, later_reach)
+    nleft = jnp.minimum(jnp.where(in_first, me, me - first_devs), most)
+    nright = jnp.minimum(jnp.where(in_first, first_devs - 1 - me, count - 1 - me), most)
+    span = jnp.where(in_first, MOST, limit)
+
+    def takes(step, there, who):
+        if isinstance(step, int) and step != later_reach:
+            return step <= there
+        far = jnp.logical_and(step == later_reach, jnp.logical_not(in_first))
+        return jnp.logical_and(step <= there, jnp.logical_or(jnp.logical_not(far), core == who))
+
     scale = width ** (-0.5)
     factor = scale * math.log2(math.e)
 
@@ -131,17 +143,16 @@
 
     pairs = ((att_k, kall), (att_v, vall))
 
-    def span(step):
-        if step == reach:
-            return pl.multiple_of(TILE + core * (TILE // 2), TILE // 2), TILE // 2
-        return pl.multiple_of(core * TILE, TILE), TILE
+    def half_of(step):
+        start = pl.multiple_of(core * TILE, TILE)
+        return start, pl.ds((reach - step) * length + start, TILE)
 
     def kv_copy(which, step):
-        start, size = span(step)
+        start, place = half_of(step)
         source, target = pairs[which]
         return pltpu.make_async_remote_copy(
-            src_ref=source.at[pl.ds(start, size)],
-            dst_ref=target.at[pl.ds((reach - step) * length + start, size)],
+            src_ref=source.at[pl.ds(start, TILE)],
+            dst_ref=target.at[place],
             send_sem=kv_send.at[which, step - 1],
             recv_sem=kv_recv.at[which, step - 1],
             device_id={"ctx": me + step},
@@ -149,9 +160,8 @@
         )
 
     def pair_copy(which, step):
-        start, size = span(step)
         target = pairs[which][1]
-        place = pl.ds((reach - step) * length + start, size)
+        place = half_of(step)[1]
         return pltpu.make_async_remote_copy(
             src_ref=target.at[place],
             dst_ref=target.at[place],
@@ -161,29 +171,79 @@
             device_id_type=MESH,
         )
 
-    def pass_on(step):
-        @pl.when(step <= nleft)
-        def _():
-            for which in range(2):
-                kv_copy(which, step).wait_recv()
-                pair_copy(which, step).start()
-
-    def state_copy(side, step):
+    def pass_on(which, steps):
+        for step in steps:
+            if step <= reach:
+
+                @pl.when(takes(step, nleft, 1))
+                def _():
+                    kv_copy(which, step).wait_recv()
+                    pair_copy(which, step).start()
+
+    def pair_wait(which):
+        for step in range(1, reach + 1):
+
+            @pl.when(takes(step, nleft, 0))
+            def _():
+                pair_copy(which, step).wait_recv()
+
+    hops = ((1, 2), (1, 4))
+
+    def state_copy(trip, side, k):
+        hop = hops[trip][k]
         return pltpu.make_async_remote_copy(
-            src_ref=snd.at[side],
-            dst_ref=got.at[side, step - 1],
-            send_sem=st_send.at[side, step - 1],
-            recv_sem=st_recv.at[side, step - 1],
-            device_id={"ctx": me + step if side == 0 else me - step},
+            src_ref=snd.at[trip, side],
+            dst_ref=got.at[trip, side, k],
+            send_sem=st_send.at[trip, side, k],
+            recv_sem=st_recv.at[trip, side, k],
+            device_id={"ctx": me + hop if side == 0 else me - hop},
             device_id_type=MESH,
         )
 
-    for step in range(1, reach + 1):
-
-        @pl.when(step <= nright)
-        def _():
-            kv_copy(0, step).start()
-            kv_copy(1, step).start()
+    def state_start(trip):
+        for k, hop in enumerate(hops[trip]):
+            for side, there in ((0, nright), (1, nleft)):
+
+                @pl.when(hop <= there)
+                def _():
+                    state_copy(trip, side, k).start()
+
+            for side, there in ((0, nleft), (1, nright)):
+
+                @pl.when(hop > there)
+                def _():
+                    got[trip, side, k] = jnp.zeros(got.shape[3:], BF16)
+
+    def state_wait(trip):
+        for k, hop in enumerate(hops[trip]):
+            for side, there in ((0, nleft), (1, nright)):
+
+                @pl.when(hop <= there)
+                def _():
+                    state_copy(trip, side, k).wait_recv()
+
+    def state_write(trip, side, totals, mults):
+        pads = []
+        for h in range(heads):
+            snd[trip, side, h * width : (h + 1) * width, :] = totals[h].astype(BF16)
+            high, low = split(jnp.broadcast_to(mults[h], (1, width)))
+            pads.append((high.astype(F32), low.astype(F32)))
+        rows16 = [pads[h][0] for h in range(heads)] + [pads[h][1] for h in range(heads)]
+        rows16.append(jnp.zeros((16 - 2 * heads, width), F32))
+        snd[trip, side, heads * width :, :] = jnp.concatenate(rows16, axis=0).astype(BF16)
+
+    def state_read(trip, side, k, h):
+        at = heads * width
+        total = got[trip, side, k, h * width : (h + 1) * width, :].astype(F32)
+        pads = got[trip, side, k, at : at + 16, :].astype(F32)
+        return total, pads[h : h + 1] + pads[heads + h : heads + h + 1]
+
+    for which in range(2):
+        for step in range(1, reach + 1):
+
+            @pl.when(takes(step, nright, 1))
+            def _():
+                kv_copy(which, step).start()
 
     for load in loads:
         load.wait()
@@ -204,6 +264,7 @@
             dol = picked[3].astype(BF16)
             states[1, b, h] = dot_nn(query_high, dol) + dot_nn(query_low, dol)
 
+    totals, mults = ([], []), ([], [])
     for h in range(heads):
         keep = [jnp.exp(head_terms(b, h)[2]) for b in range(nblocks)]
         total_l = states[0, 0, h]
@@ -217,13 +278,25 @@
             total_r = states[1, b, h] + keep[b] * precedes[b] * total_r
             mult_r = mult_r * keep[b] * precedes[b]
         for side, total, mult in ((0, total_l, mult_l), (1, total_r, mult_r)):
-            high, low = split(jnp.broadcast_to(mult, (16, width)))
-            snd[side, h, 0:width, :] = total.astype(BF16)
-            snd[side, h, width : width + 16, :] = high
-            snd[side, h, width + 16 : width + 32, :] = low
-
-    pass_on(1)
-    pass_on(2)
+            totals[side].append(total)
+            mults[side].append(mult)
+            local[side, h] = total
+    for side in range(2):
+        state_write(0, side, totals[side], mults[side])
+
+    def state_join():
+        state_wait(0)
+        for side in range(2):
+            joined, spans = [], []
+            for h in range(heads):
+                one, mult_one = state_read(0, side, 0, h)
+                two, mult_two = state_read(0, side, 1, h)
+                joined.append(local[side, h] + mults[side][h] * (one + mult_one * two))
+                spans.append(mults[side][h] * mult_one * mult_two)
+            state_write(1, side, joined, spans)
+        state_start(1)
+
+    pass_on(0, (1, 2))
 
     def within(b):
         for h in range(heads):
@@ -238,32 +311,11 @@
             grads[2, b, h] = dot_nn(right, dol)
 
     within(0)
-    pass_on(3)
-    pass_on(4)
+    pass_on(0, (3, 4))
     for b in range(1, nblocks):
         within(b)
-    pass_on(5)
-    pass_on(6)
-
-    for step in range(1, reach + 1):
-        for side, there in ((0, nright), (1, nleft)):
-
-            @pl.when(step <= there)
-            def _():
-                state_copy(side, step).start()
-
-        for side, there in ((0, nleft), (1, nright)):
-
-            @pl.when(step > there)
-            def _():
-                got[side, step - 1] = jnp.zeros(got.shape[2:], BF16)
-
-    for step in range(1, reach + 1):
-
-        @pl.when(step <= nleft)
-        def _():
-            for which in range(2):
-                pair_copy(which, step).wait_recv()
+    pass_on(0, (5, 6))
+    pair_wait(0)
 
     def rows_of(j):
         return pl.ds(pl.multiple_of(j * TILE, TILE), TILE)
@@ -313,7 +365,7 @@
 
     def attend(b):
         diag = base + b
-        first = jnp.maximum(b + 1, base - nblocks * nleft)
+        first = jnp.maximum(base + b + 1 - span, base - nblocks * nleft)
         queries = q[b * chunk : (b + 1) * chunk, :]
         douts = dout[b * chunk : (b + 1) * chunk, :]
         here = doc[me * nblocks + b]
@@ -326,25 +378,29 @@
             flipped[j] = kall[rows_of(j), :].astype(F32).T.astype(BF16)
 
         s = jnp.where(seen_q, dot_nt(kall[rows_of(diag), :], queries), NEG)
-        scores[diag - b - 1] = s
+        scores[diag - first] = s
         flip(diag)
 
         def find_max(j, top):
             s = dot_nt(kall[rows_of(j), :], queries)
-            scores[j - b - 1] = s
+            scores[j - first] = s
             if b == 0:
                 flip(j)
             return jnp.maximum(top, folded(s, jnp.max) - hidden(j))
 
         top = lax.fori_loop(first, diag, find_max, folded(s, jnp.max))
         top = jnp.max(top, axis=0, keepdims=True) * factor
+        if b == 0:
+            pass_on(1, range(1, reach + 1))
+            pair_wait(1)
+            state_start(0)
 
         def sums(j, carried):
             amount, weighted = carried
-            p = jnp.exp2(scores[j - b - 1] * factor - (top + hidden(j)))
+            p = jnp.exp2(scores[j - first] * factor - (top + hidden(j)))
             g = dot_nt(vall[rows_of(j), :], douts)
-            scores[j - b - 1] = p
-            probs_grad[j - b - 1] = g
+            scores[j - first] = p
+            probs_grad[j - first] = g
             return amount + folded(p, jnp.sum), weighted + folded(p * g, jnp.sum)
 
         zero = jnp.zeros((8, chunk), F32)
@@ -353,8 +409,8 @@
         delta = jnp.sum(weighted, axis=0, keepdims=True) * inverse
 
         def one(j, acc):
-            p = scores[j - b - 1] * inverse
-            g = p * (probs_grad[j - b - 1] - delta)
+            p = scores[j - first] * inverse
+            g = p * (probs_grad[j - first] - delta)
             p = p.astype(BF16)
             g = g.astype(BF16)
             at = rows_of(j)
@@ -370,7 +426,7 @@
         if b == 0:
             acc = lax.fori_loop(first, diag + 1, one, acc)
         else:
-            last = jnp.minimum(nleft, reach - 1)
+            last = jnp.minimum(nleft, jnp.where(in_first, reach, later_reach - 1))
 
             def by_step(i, acc):
                 step = last - i
@@ -389,36 +445,26 @@
         att_dq[b * chunk : (b + 1) * chunk, :] = (acc.T * scale).astype(BF16)
 
     attend(0)
-    far = nleft == reach
+    state_join()
+    far = jnp.logical_and(jnp.logical_not(in_first), nleft == later_reach)
 
     @pl.when(jnp.logical_and(far, core == 0))
     def _():
         for which in range(2):
-            grad_copy(which, reach).start()
+            grad_copy(which, later_reach).start()
 
     @pl.when(jnp.logical_and(far, core == 1))
     def _():
-        send_home(reach)
+        send_home(later_reach)
 
     attend(1)
-
-    for side, there in ((0, nleft), (1, nright)):
-        for step in range(1, reach + 1):
-
-            @pl.when(step <= there)
-            def _():
-                state_copy(side, step).wait_recv()
+    state_wait(1)
 
     for h in range(heads):
         ends = []
         for side in range(2):
-            state = jnp.zeros((width, width), F32)
-            for step in range(reach, 0, -1):
-                mult = (
-                    got[side, step - 1, h, width : width + 16, :].astype(F32)[0:1]
-                    + got[side, step - 1, h, width + 16 : width + 32, :].astype(F32)[0:1]
-                )
-                state = got[side, step - 1, h, 0:width, :].astype(F32) + mult * state
+            near, mult = state_read(1, side, 0, h)
+            state = near + mult * state_read(1, side, 1, h)[0]
             ends.append(state)
         keep = [jnp.exp(head_terms(b, h)[2]) for b in range(nblocks)]
         state = ends[0]
@@ -456,11 +502,6 @@
         grad_copy(which, 0).wait_recv()
         paired[which, 0] = mine(which, 0)
 
-    def takes(step, there, who):
-        if step < reach:
-            return step <= there
-        return jnp.logical_and(step <= there, core == who)
-
     for step in range(1, reach + 1):
 
         @pl.when(takes(step, nright, 1))
@@ -474,53 +515,81 @@
 
     for which in range(2):
         grad_copy(which, 0).wait_send()
+    for trip in range(2):
+        for k, hop in enumerate(hops[trip]):
+            for side, there in ((0, nright), (1, nleft)):
+
+                @pl.when(hop <= there)
+                def _():
+                    state_copy(trip, side, k).wait_send()
+
     for step in range(1, reach + 1):
 
-        @pl.when(step <= nright)
+        @pl.when(takes(step, nright, 1))
         def _():
             for which in range(2):
                 kv_copy(which, step).wait_send()
-            state_copy(0, step).wait_send()
-
-        @pl.when(step <= nleft)
+
+        @pl.when(takes(step, nleft, 1))
         def _():
             for which in range(2):
                 pair_copy(which, step).wait_send()
-            state_copy(1, step).wait_send()
+            home_copy(step).wait_send()
 
         @pl.when(takes(step, nleft, 0))
         def _():
             for which in range(2):
                 grad_copy(which, step).wait_send()
 
-        @pl.when(takes(step, nleft, 1))
-        def _():
-            home_copy(step).wait_send()
-
-
-def shards(count, lin_q, lin_k, lin_v, lin_dout, lin_decay, att_q, att_k, att_v, att_dout, doc_block):
-    length, heads, width = lin_q.shape
-    nblocks = length // TILE
-    assert nblocks == 2
-    reach = -(-(MOST - 1) // nblocks)
-    rows = length * heads
-    window = (reach + 1) * length
-    flat = lambda x: x.reshape(rows, width)
-    outs = pl.pallas_call(
-        functools.partial(whole_kernel, count, reach, heads, nblocks),
+
+def slots_of(limit, nblocks):
+    return max(MOST // nblocks - 1, limit // nblocks)
+
+
+def place_kernel(*refs):
+    half = (len(refs) - 1) // 2
+    sems = refs[-1]
+    moves = [
+        pltpu.make_async_copy(refs[i], refs[half + i], sems.at[i]) for i in range(half)
+    ]
+    for move in moves:
+        move.start()
+    for move in moves:
+        move.wait()
+
+
+def place(outs):
+    return pl.pallas_call(
+        place_kernel,
+        out_shape=[SHAPE(x.shape, x.dtype) for x in outs],
+        in_specs=[ANYWHERE] * len(outs),
+        out_specs=[ANYWHERE] * len(outs),
+        scratch_shapes=[DMA((len(outs),))],
+        name="place",
+    )(*outs)
+
+
+def call_whole(count, limit, heads, nblocks, args):
+    width = args[-1].shape[1]
+    rows = nblocks * TILE * heads
+    reach = slots_of(limit, nblocks)
+    window = (reach + 1) * nblocks * TILE
+    return pl.pallas_call(
+        functools.partial(whole_kernel, count, limit, heads, nblocks),
         out_shape=[SHAPE((rows, width), BF16)] * 4 + [SHAPE((TILE, width), BF16)] * 2,
         in_specs=[IN_SMEM] + [ANYWHERE] * 9,
         out_specs=[IN_VMEM] * 6,
         scratch_shapes=[
             pltpu.VMEM((4, TILE * heads, width), F32),
             pltpu.VMEM((4, rows, width), BF16),
-            pltpu.VMEM(lin_decay.shape, F32),
+            pltpu.VMEM((heads, nblocks * TILE), F32),
             pltpu.VMEM((rows, width), BF16),
             pltpu.VMEM((rows, width), BF16),
             pltpu.VMEM((window, width), BF16),
             pltpu.VMEM((window, width), BF16),
             pltpu.VMEM((4, nblocks, heads, TILE, width), BF16),
             pltpu.VMEM((2, nblocks, heads, width, width), F32),
+            pltpu.VMEM((2, heads, width, width), F32),
             pltpu.VMEM((3, nblocks, heads, TILE, width), F32),
             pltpu.VMEM((3, rows, width), F32),
             pltpu.VMEM((MOST, TILE, TILE * heads), F32),
@@ -528,8 +597,8 @@
             pltpu.VMEM((window // TILE, width, TILE), BF16),
             pltpu.VMEM((window, width), F32),
             pltpu.VMEM((window, width), F32),
-            pltpu.VMEM((2, heads, width + 32, width), BF16),
-            pltpu.VMEM((2, reach, heads, width + 32, width), BF16),
+            pltpu.VMEM((2, 2, heads * width + 16, width), BF16),
+            pltpu.VMEM((2, 2, 2, heads * width + 16, width), BF16),
             pltpu.VMEM((2, reach + 1, TILE, width), F32),
             pltpu.VMEM((reach, 2, TILE, width), BF16),
             pltpu.VMEM((reach, 2, TILE, width), BF16),
@@ -538,21 +607,40 @@
             DMA((2, reach)),
             DMA((2, reach)),
             DMA((2, reach)),
-            DMA((2, reach)),
-            DMA((2, reach)),
+            DMA((2, 2, 2)),
+            DMA((2, 2, 2)),
             DMA((2, reach + 1)),
             DMA((2, reach + 1)),
             DMA((reach,)),
             DMA((reach,)),
         ],
         compiler_params=pltpu.CompilerParams(
-            collective_id=0, has_side_effects=True, vmem_limit_bytes=VMEM_LIMIT
+            collective_id=0 if limit == MOST else 1,
+            has_side_effects=True,
+            vmem_limit_bytes=VMEM_LIMIT,
         ),
-        name="whole",
-    )(
+        name="whole_%d" % limit,
+    )(*args)
+
+
+def shards(count, lin_q, lin_k, lin_v, lin_dout, lin_decay, att_q, att_k, att_v, att_dout, doc_block):
+    length, heads, width = lin_q.shape
+    nblocks = length // TILE
+    assert nblocks == 2
+    flat = lambda x: x.reshape(length * heads, width)
+    args = (
         doc_block, flat(lin_q), flat(lin_k), flat(lin_v), flat(lin_dout), lin_decay,
         flat(att_q), flat(att_dout), att_k, att_v,
     )
+    later = doc_block[MOST:]
+    long = jnp.any(later[SHORT:] == later[:-SHORT])
+    outs = lax.cond(
+        long,
+        lambda *a: call_whole(count, MOST, heads, nblocks, a),
+        lambda *a: call_whole(count, SHORT, heads, nblocks, a),
+        *args,
+    )
+    outs = place(outs)
     full = lambda x: x.reshape(length, heads, width)
     return (full(outs[0]), full(outs[1]), full(outs[2]), full(outs[3]), outs[4], outs[5])
 

time: 76 us -> 57.5 us (0.76)
  the two profiles are of different devices: /device:TPU:22 before, /device:TPU:6 now
where the time goes in v2:
time: 57.5 us; the launch traced here: 57.3 us
  Pallas kernels  53.5 us (93%)
  between operations  1.5 us (3%)
  other arithmetic  1.44 us (3%)
  local copies, waits for them, and re-layouts  0.64 us (1%)
    pallas_call x1, Pallas kernels, call_whole(): pl.pallas_call(functools.partial(whole_kernel, count, limit, heads, nbloc...  52.1 us
    reduce_or x1, other arithmetic, shards(): long = jnp.any(later[SHORT:] == later[:-SHORT])  1.44 us
    pallas_call x1, Pallas kernels, place(): pl.pallas_call(place_kernel, out_shape=[SHAPE(x.shape, x.dtype) for x in...  1.4 us

profile of v2, /device:TPU:6, one launch (start us, length us, event | category | flops | bytes accessed | tf_op | source)
XLA Modules:
  0.0 57.3 jit_solution(5392350495652443148)
XLA Ops:
  0.6 0.0 copy-start
  0.6 1.4 %compare_reduce_fusion = pred[]{:T(512)} fusion(s32[32]{0:T(128)} %param.21), kind=kLoop, calls=%fused_computation | loop fusion | flops 23 | bytes 97 | tf_op jit(solution)/shard_map/reduce_or | solution.py:636
  2.7 0.0 copy-start.1
  2.7 0.0 copy-done
  2.8 0.6 %copy-done.1 = s32[32]{0:T(128)S(1)} copy-done((s32[32]{0:T(128)S(1)}, s32[32]{0:T(128)}, u32[]{:S(2)}) %copy-start.1) | copy-done | bytes 152
  3.4 52.3 %conditional.1 = ((bf16[2048,128]{1,0:T(8,128)(2,1)S(1)}, bf16[2048,128]{1,0:T(8,128)(2,1)S(1)}, bf16[2048,128]{1,0:T(8,128)(2,1)S(1)}, bf16[2048,128]{1,0:T(8,1...) conditional(s32[]{:T(128)} %convert_element_type.3, (s32[32]{0:T(128)S(1)}, ...), branch_computations={%region_1.0_spmd, %region_2.0_spmd} | conditional | bytes 8 | solution.py:637
  3.4 52.1 %whole_8.1 = (bf16[2048,128]{1,0:T(8,128)(2,1)S(1)}, bf16[2048,128]{1,0:T(8,128)(2,1)S(1)}, bf16[2048,128]{1,0:T(8,128)(2,1)S(1)}, bf16[2048,128]{1,0:T(8,128)(2...) custom-call(s32[32]{0:T(128)S(1)} %get-tuple-element.40.doc, ...), custom_call_target="tpu_custom_call" | custom-call | tf_op jit(solution)/shard_map/cond/branch_0_fun/whole_8/pallas_call | solution.py:577
  55.7 1.4 %place.1 = (bf16[2048,128]{1,0:T(8,128)(2,1)}, bf16[2048,128]{1,0:T(8,128)(2,1)}, bf16[2048,128]{1,0:T(8,128)(2,1)}, bf16[2048,128]{1,0:T(8,128)(2,1)}, bf16[256...) custom-call(bf16[2048,128]{1,0:T(8,128)(2,1)S(1)} %get-tuple-element.78.refs_0_, ...), custom_call_target="tpu_custom_call" | custom-call | tf_op jit(solution)/shard_map/place/pallas_call | solution.py:562
Async XLA Ops:
  0.6 2.1 %copy-start = (f32[4,512]{1,0:T(4,128)S(1)}, f32[4,512]{1,0:T(4,128)}, u32[]{:S(2)}) copy-start(f32[4,512]{1,0:T(4,128)} %param.16) | copy-start | bytes 24580
  2.7 0.7 %copy-start.1 = (s32[32]{0:T(128)S(1)}, s32[32]{0:T(128)}, u32[]{:S(2)}) copy-start(s32[32]{0:T(128)} %param.21) | copy-start | bytes 388

commit v3 on v2

--- a/solution.py
+++ b/solution.py
@@ -20,7 +20,7 @@
 IN_VMEM = pl.BlockSpec(memory_space=pltpu.VMEM)
 IN_SMEM = pl.BlockSpec(memory_space=pltpu.SMEM)
 ANYWHERE = pl.BlockSpec(memory_space=pl.ANY)
-VMEM_LIMIT = 60 * 1024 * 1024
+VMEM_LIMIT = 62 * 1024 * 1024
 
 
 def dot_nn(a, b):
@@ -86,12 +86,13 @@
     doc, lq, lk, lv, ld, dec_in, aq, ado, att_k, att_v,
     lin_dq, lin_dk, lin_dv, att_dq, att_dk, att_dv,
     wide, raw, dec, q, dout, kall, vall, parts, states, local, grads, mixed,
-    scores, probs_grad, flipped, dkey, dvalue,
+    scores, probs_grad, peaks, top_ref, amount_ref, weighted_ref, dq_sum, flipped, dkey, dvalue,
     snd, got, paired, out, inbox,
     raw_sem, kv_send, kv_recv, pair_send, pair_recv, st_send, st_recv,
     pg_send, pg_recv, home_send, home_recv,
 ):
     me = lax.axis_index("ctx")
+    carry = (top_ref, amount_ref, weighted_ref)
     core = lax.axis_index("head")
     length = nblocks * TILE
     width = lq.shape[1]
@@ -171,21 +172,16 @@
             device_id_type=MESH,
         )
 
-    def pass_on(which, steps):
-        for step in steps:
-            if step <= reach:
-
-                @pl.when(takes(step, nleft, 1))
-                def _():
-                    kv_copy(which, step).wait_recv()
-                    pair_copy(which, step).start()
-
-    def pair_wait(which):
-        for step in range(1, reach + 1):
-
-            @pl.when(takes(step, nleft, 0))
-            def _():
-                pair_copy(which, step).wait_recv()
+    def pass_on(step):
+        @pl.when(takes(step, nleft, 1))
+        def _():
+            for which in range(2):
+                kv_copy(which, step).wait_recv()
+                pair_copy(which, step).start()
+
+    def pair_wait(step):
+        for which in range(2):
+            pair_copy(which, step).wait_recv()
 
     hops = ((1, 2), (1, 4))
 
@@ -200,27 +196,29 @@
             device_id_type=MESH,
         )
 
-    def state_start(trip):
+    def sent(side):
+        return nright if side == 0 else nleft
+
+    def due(side):
+        return nleft if side == 0 else nright
+
+    def state_start(trip, side):
         for k, hop in enumerate(hops[trip]):
-            for side, there in ((0, nright), (1, nleft)):
-
-                @pl.when(hop <= there)
-                def _():
-                    state_copy(trip, side, k).start()
-
-            for side, there in ((0, nleft), (1, nright)):
-
-                @pl.when(hop > there)
-                def _():
-                    got[trip, side, k] = jnp.zeros(got.shape[3:], BF16)
-
-    def state_wait(trip):
+
+            @pl.when(hop <= sent(side))
+            def _():
+                state_copy(trip, side, k).start()
+
+            @pl.when(hop > due(side))
+            def _():
+                got[trip, side, k] = jnp.zeros(got.shape[3:], BF16)
+
+    def state_wait(trip, side):
         for k, hop in enumerate(hops[trip]):
-            for side, there in ((0, nleft), (1, nright)):
-
-                @pl.when(hop <= there)
-                def _():
-                    state_copy(trip, side, k).wait_recv()
+
+            @pl.when(hop <= due(side))
+            def _():
+                state_copy(trip, side, k).wait_recv()
 
     def state_write(trip, side, totals, mults):
         pads = []
@@ -238,11 +236,11 @@
         pads = got[trip, side, k, at : at + 16, :].astype(F32)
         return total, pads[h : h + 1] + pads[heads + h : heads + h + 1]
 
-    for which in range(2):
-        for step in range(1, reach + 1):
-
-            @pl.when(takes(step, nright, 1))
-            def _():
+    for step in range(1, reach + 1):
+
+        @pl.when(takes(step, nright, 1))
+        def _():
+            for which in range(2):
                 kv_copy(which, step).start()
 
     for load in loads:
@@ -284,19 +282,19 @@
     for side in range(2):
         state_write(0, side, totals[side], mults[side])
 
-    def state_join():
-        state_wait(0)
-        for side in range(2):
-            joined, spans = [], []
-            for h in range(heads):
-                one, mult_one = state_read(0, side, 0, h)
-                two, mult_two = state_read(0, side, 1, h)
-                joined.append(local[side, h] + mults[side][h] * (one + mult_one * two))
-                spans.append(mults[side][h] * mult_one * mult_two)
-            state_write(1, side, joined, spans)
-        state_start(1)
-
-    pass_on(0, (1, 2))
+    state_start(0, 1)
+
+    def state_join(side):
+        state_wait(0, side)
+        joined, spans = [], []
+        for h in range(heads):
+            one, mult_one = state_read(0, side, 0, h)
+            two, mult_two = state_read(0, side, 1, h)
+            joined.append(local[side, h] + mults[side][h] * (one + mult_one * two))
+            spans.append(mults[side][h] * mult_one * mult_two)
+        state_write(1, side, joined, spans)
+        state_start(1, side)
+
 
     def within(b):
         for h in range(heads):
@@ -311,12 +309,9 @@
             grads[2, b, h] = dot_nn(right, dol)
 
     within(0)
-    pass_on(0, (3, 4))
+    pass_on(1)
     for b in range(1, nblocks):
         within(b)
-    pass_on(0, (5, 6))
-    pair_wait(0)
-
     def rows_of(j):
         return pl.ds(pl.multiple_of(j * TILE, TILE), TILE)
 
@@ -355,116 +350,172 @@
 
     chunk = rows
     base = reach * nblocks
+    offset = offset_of(limit, nblocks)
+    near = jnp.minimum(nleft, jnp.where(in_first, reach, later_reach - 1))
+    far = jnp.logical_and(jnp.logical_not(in_first), nleft == later_reach)
+    far_tile = (reach - later_reach) * nblocks + 1
+    queries = [q[b * chunk : (b + 1) * chunk, :] for b in range(nblocks)]
+    douts = [dout[b * chunk : (b + 1) * chunk, :] for b in range(nblocks)]
     dkey[rows_of(base + 1), :] = jnp.zeros((TILE, width), F32)
     dvalue[rows_of(base + 1), :] = jnp.zeros((TILE, width), F32)
-    token = lax.broadcasted_iota(jnp.int32, (TILE, chunk), 1) // heads
-    seen_q = lax.broadcasted_iota(jnp.int32, (TILE, chunk), 0) <= token
+
+    def keys_at(j, n):
+        return pl.ds(pl.multiple_of(j * TILE, TILE), n * TILE)
+
+    def hidden(b, j):
+        at = jnp.clip(me * nblocks - base + j, 0, count * nblocks - 1)
+        return jnp.where(doc[at] == doc[me * nblocks + b], 0.0, -NEG).astype(F32)
 
     def folded(x, op):
         return op(x.reshape(TILE // 8, 8, chunk), axis=0)
 
-    def attend(b):
-        diag = base + b
-        first = jnp.maximum(base + b + 1 - span, base - nblocks * nleft)
-        queries = q[b * chunk : (b + 1) * chunk, :]
-        douts = dout[b * chunk : (b + 1) * chunk, :]
-        here = doc[me * nblocks + b]
-
-        def hidden(j):
-            at = jnp.clip(me * nblocks - base + j, 0, count * nblocks - 1)
-            return jnp.where(doc[at] == here, 0.0, -NEG).astype(F32)
-
-        def flip(j):
-            flipped[j] = kall[rows_of(j), :].astype(F32).T.astype(BF16)
-
-        s = jnp.where(seen_q, dot_nt(kall[rows_of(diag), :], queries), NEG)
-        scores[diag - first] = s
-        flip(diag)
-
-        def find_max(j, top):
-            s = dot_nt(kall[rows_of(j), :], queries)
-            scores[j - first] = s
-            if b == 0:
-                flip(j)
-            return jnp.maximum(top, folded(s, jnp.max) - hidden(j))
-
-        top = lax.fori_loop(first, diag, find_max, folded(s, jnp.max))
-        top = jnp.max(top, axis=0, keepdims=True) * factor
-        if b == 0:
-            pass_on(1, range(1, reach + 1))
-            pair_wait(1)
-            state_start(0)
-
-        def sums(j, carried):
-            amount, weighted = carried
-            p = jnp.exp2(scores[j - first] * factor - (top + hidden(j)))
-            g = dot_nt(vall[rows_of(j), :], douts)
-            scores[j - first] = p
-            probs_grad[j - first] = g
-            return amount + folded(p, jnp.sum), weighted + folded(p * g, jnp.sum)
-
-        zero = jnp.zeros((8, chunk), F32)
-        amount, weighted = lax.fori_loop(first, diag + 1, sums, (zero, zero))
+    def causal():
+        token = lax.broadcasted_iota(jnp.int32, (TILE, chunk), 1) // heads
+        return lax.broadcasted_iota(jnp.int32, (TILE, chunk), 0) <= token
+
+    def flip(step, tiles):
+        first = (reach - step) * nblocks + tiles[0]
+        low = tiles[0] * TILE
+        block = kall[keys_at(first, len(tiles)), :].astype(F32).T.astype(BF16)
+        flipped[step, :, low : low + len(tiles) * TILE] = block
+
+    def weigh(b, step, tiles, carried, diag=False):
+        top, amount, weighted = carried
+        first = (reach - step) * nblocks + tiles[0]
+        at = keys_at(first, len(tiles))
+        s = dot_nt(kall[at, :], queries[b]) * factor
+        g = dot_nt(vall[at, :], douts[b])
+        parts_s = [s[k * TILE : (k + 1) * TILE] for k in range(len(tiles))]
+        shades = [hidden(b, first + k) for k in range(len(tiles))]
+        if diag:
+            parts_s[-1] = jnp.where(causal(), parts_s[-1], NEG)
+        peak = folded(parts_s[0], jnp.max) - shades[0]
+        for k in range(1, len(tiles)):
+            peak = jnp.maximum(peak, folded(parts_s[k], jnp.max) - shades[k])
+        peak = jnp.maximum(top, jnp.max(peak, axis=0, keepdims=True))
+        shrink = jnp.exp2(top - peak)
+        amount = amount * shrink
+        weighted = weighted * shrink
+        for k in range(len(tiles)):
+            p = jnp.exp2(parts_s[k] - (peak + shades[k]))
+            gk = g[k * TILE : (k + 1) * TILE]
+            scores[first + k - offset] = p
+            probs_grad[first + k - offset] = gk
+            amount += folded(p, jnp.sum)
+            weighted += folded(p * gk, jnp.sum)
+        peaks[b, step] = peak
+        return peak, amount, weighted
+
+    def ready(carried):
+        top, amount, weighted = carried
         inverse = 1.0 / jnp.sum(amount, axis=0, keepdims=True)
         delta = jnp.sum(weighted, axis=0, keepdims=True) * inverse
-
-        def one(j, acc):
-            p = scores[j - first] * inverse
-            g = p * (probs_grad[j - first] - delta)
-            p = p.astype(BF16)
-            g = g.astype(BF16)
-            at = rows_of(j)
-            if b == 0:
-                dvalue[at, :] = dot_nn(p, douts)
-                dkey[at, :] = dot_nn(g, queries)
-            else:
-                dvalue[at, :] += dot_nn(p, douts)
-                dkey[at, :] += dot_nn(g, queries)
-            return acc + dot_nn(flipped[j], g)
-
-        acc = jnp.zeros((width, chunk), F32)
+        return top, inverse, delta
+
+    def grade(b, step, tiles, stats, acc):
+        top, inverse, delta = stats
+        first = (reach - step) * nblocks + tiles[0]
+        low = tiles[0] * TILE
+        size = len(tiles) * TILE
+        held = pl.ds(first - offset, len(tiles))
+        p = scores[held].reshape(size, chunk) * (jnp.exp2(peaks[b, step] - top) * inverse)
+        g = p * (probs_grad[held].reshape(size, chunk) - delta)
+        p = p.astype(BF16)
+        g = g.astype(BF16)
+        at = keys_at(first, len(tiles))
         if b == 0:
-            acc = lax.fori_loop(first, diag + 1, one, acc)
+            dvalue[at, :] = dot_nn(p, douts[b])
+            dkey[at, :] = dot_nn(g, queries[b])
         else:
-            last = jnp.minimum(nleft, jnp.where(in_first, reach, later_reach - 1))
-
-            def by_step(i, acc):
-                step = last - i
-                j = (reach - step) * nblocks
-                acc = one(j + 1, one(j, acc))
-                for which in range(2):
-                    grad_copy(which, step).start()
-
-                @pl.when(i > 0)
-                def _():
-                    send_home(step + 1)
-
-                return acc
-
-            acc = lax.fori_loop(0, last + 1, by_step, acc)
+            dvalue[at, :] += dot_nn(p, douts[b])
+            dkey[at, :] += dot_nn(g, queries[b])
+        return acc + dot_nn(flipped[step, :, low : low + size], g)
+
+    def finish(b, acc):
         att_dq[b * chunk : (b + 1) * chunk, :] = (acc.T * scale).astype(BF16)
 
-    attend(0)
-    state_join()
-    far = jnp.logical_and(jnp.logical_not(in_first), nleft == later_reach)
-
-    @pl.when(jnp.logical_and(far, core == 0))
+    flip(0, (0, 1))
+    row = jnp.zeros((8, chunk), F32)
+    start = (jnp.full((1, chunk), NEG, F32), row, row)
+    state_zero = weigh(0, 0, (0,), start, diag=True)
+    for i, ref in enumerate(carry):
+        ref[...] = state_zero[i]
+
+    def first_pass(step, carried):
+        pass_on(step + 1)
+        pair_wait(step)
+        flip(step, (0, 1))
+        return weigh(0, step, (0, 1), carried)
+
+    carried = lax.fori_loop(1, near + 1, first_pass, state_zero)
+    for i, ref in enumerate(carry):
+        ref[...] = carried[i]
+
+    @pl.when(far)
     def _():
-        for which in range(2):
-            grad_copy(which, later_reach).start()
+        @pl.when(core == 0)
+        def _():
+            pair_wait(later_reach)
+
+        flip(later_reach, (1,))
+        more = weigh(0, later_reach, (1,), tuple(ref[...] for ref in carry))
+        for i, ref in enumerate(carry):
+            ref[...] = more[i]
+
+    state_join(1)
+    state_start(0, 0)
+
+    stats = ready(tuple(ref[...] for ref in carry))
+    acc = grade(0, 0, (0,), stats, jnp.zeros((width, chunk), F32))
+    carried = weigh(1, 0, (0, 1), start, diag=True)
+
+    def both(step, packed):
+        carried, acc = packed
+        acc = grade(0, step, (0, 1), stats, acc)
+        return weigh(1, step, (0, 1), carried), acc
+
+    carried, acc = lax.fori_loop(1, near + 1, both, (carried, acc))
+    dq_sum[...] = acc
+
+    @pl.when(far)
+    def _():
+        dq_sum[...] = grade(0, later_reach, (1,), stats, dq_sum[...])
+
+        @pl.when(core == 0)
+        def _():
+            for which in range(2):
+                grad_copy(which, later_reach).start()
+
+    finish(0, dq_sum[...])
+    state_join(0)
 
     @pl.when(jnp.logical_and(far, core == 1))
     def _():
         send_home(later_reach)
 
-    attend(1)
-    state_wait(1)
+    last_stats = ready(carried)
+
+    def last_pass(i, acc):
+        step = near - i
+        acc = grade(1, step, (0, 1), last_stats, acc)
+        for which in range(2):
+            grad_copy(which, step).start()
+
+        @pl.when(i > 0)
+        def _():
+            send_home(step + 1)
+
+        return acc
+
+    finish(1, lax.fori_loop(0, near + 1, last_pass, jnp.zeros((width, chunk), F32)))
+    for side in range(2):
+        state_wait(1, side)
 
     for h in range(heads):
         ends = []
         for side in range(2):
-            near, mult = state_read(1, side, 0, h)
-            state = near + mult * state_read(1, side, 1, h)[0]
+            close, mult = state_read(1, side, 0, h)
+            state = close + mult * state_read(1, side, 1, h)[0]
             ends.append(state)
         keep = [jnp.exp(head_terms(b, h)[2]) for b in range(nblocks)]
         state = ends[0]
@@ -546,6 +597,10 @@
     return max(MOST // nblocks - 1, limit // nblocks)
 
 
+def offset_of(limit, nblocks):
+    return max(0, slots_of(limit, nblocks) * nblocks + 1 - MOST)
+
+
 def place_kernel(*refs):
     half = (len(refs) - 1) // 2
     sems = refs[-1]
@@ -574,6 +629,7 @@
     rows = nblocks * TILE * heads
     reach = slots_of(limit, nblocks)
     window = (reach + 1) * nblocks * TILE
+    held = (reach + 1) * nblocks - offset_of(limit, nblocks)
     return pl.pallas_call(
         functools.partial(whole_kernel, count, limit, heads, nblocks),
         out_shape=[SHAPE((rows, width), BF16)] * 4 + [SHAPE((TILE, width), BF16)] * 2,
@@ -592,9 +648,14 @@
             pltpu.VMEM((2, heads, width, width), F32),
             pltpu.VMEM((3, nblocks, heads, TILE, width), F32),
             pltpu.VMEM((3, rows, width), F32),
-            pltpu.VMEM((MOST, TILE, TILE * heads), F32),
-            pltpu.VMEM((MOST, TILE, TILE * heads), F32),
-            pltpu.VMEM((window // TILE, width, TILE), BF16),
+            pltpu.VMEM((held, TILE, TILE * heads), F32),
+            pltpu.VMEM((held, TILE, TILE * heads), F32),
+            pltpu.VMEM((nblocks, reach + 1, 1, TILE * heads), F32),
+            pltpu.VMEM((1, TILE * heads), F32),
+            pltpu.VMEM((8, TILE * heads), F32),
+            pltpu.VMEM((8, TILE * heads), F32),
+            pltpu.VMEM((width, TILE * heads), F32),
+            pltpu.VMEM((reach + 1, width, nblocks * TILE), BF16),
             pltpu.VMEM((window, width), F32),
             pltpu.VMEM((window, width), F32),
             pltpu.VMEM((2, 2, heads * width + 16, width), BF16),

time: 57.5 us -> 68 us (1.18)
  Pallas kernels: 53.5 us -> 64.1 us
    pallas_call x1, Pallas kernels: 1.4 us -> 17 us  [place(): pl.pallas_call(place_kernel, out_shape=[SHAPE(x.shape, x.dtype) for x in...]
    pallas_call x1, Pallas kernels: 52.1 us -> 47 us  [call_whole(): pl.pallas_call(functools.partial(whole_kernel, count, limit, heads, nbloc...]
where the time goes in v3:
time: 68 us; the launch traced here: 67.8 us
  Pallas kernels  64.1 us (94%)
  between operations  1.48 us (2%)
  other arithmetic  1.44 us (2%)
    pallas_call x1, Pallas kernels, call_whole(): pl.pallas_call(functools.partial(whole_kernel, count, limit, heads, nbloc...  47 us
    pallas_call x1, Pallas kernels, place(): pl.pallas_call(place_kernel, out_shape=[SHAPE(x.shape, x.dtype) for x in...  17 us
    reduce_or x1, other arithmetic, shards(): long = jnp.any(later[SHORT:] == later[:-SHORT])  1.44 us

profile of v3, /device:TPU:6, one launch (start us, length us, event | category | flops | bytes accessed | tf_op | source)
XLA Modules:
  0.0 67.8 jit_solution(9625303269140991812)
XLA Ops:
  0.6 0.0 copy-start
  0.6 1.4 %compare_reduce_fusion = pred[]{:T(512)} fusion(s32[32]{0:T(128)} %param.21), kind=kLoop, calls=%fused_computation | loop fusion | flops 23 | bytes 97 | tf_op jit(solution)/shard_map/reduce_or | solution.py:697
  2.7 0.0 copy-start.1
  2.7 0.0 copy-done
  2.8 0.6 copy-done.1
  3.4 47.2 %conditional.1 = ((bf16[2048,128]{1,0:T(8,128)(2,1)S(1)}, bf16[2048,128]{1,0:T(8,128)(2,1)S(1)}, bf16[2048,128]{1,0:T(8,128)(2,1)S(1)}, bf16[2048,128]{1,0:T(8,1...) conditional(s32[]{:T(128)} %convert_element_type.3, (s32[32]{0:T(128)S(1)}, ...), branch_computations={%region_1.0_spmd, %region_2.0_spmd} | conditional | bytes 8 | solution.py:698
  3.4 47.0 %whole_8.1 = (bf16[2048,128]{1,0:T(8,128)(2,1)S(1)}, bf16[2048,128]{1,0:T(8,128)(2,1)S(1)}, bf16[2048,128]{1,0:T(8,128)(2,1)S(1)}, bf16[2048,128]{1,0:T(8,128)(2...) custom-call(s32[32]{0:T(128)S(1)} %get-tuple-element.40.doc, bf16[2048,128]{1,0:T(8,128)(2,1)} %get-tuple-element.41.lq, ...), custom_call_target="tpu_custom_call" | custom-call | tf_op jit(solution)/shard_map/cond/branch_0_fun/whole_8/pallas_call | solution.py:633
  50.6 17.0 %place.1 = (bf16[2048,128]{1,0:T(8,128)(2,1)}, bf16[2048,128]{1,0:T(8,128)(2,1)}, bf16[2048,128]{1,0:T(8,128)(2,1)}, bf16[2048,128]{1,0:T(8,128)(2,1)}, bf16[256...) custom-call(bf16[2048,128]{1,0:T(8,128)(2,1)S(1)} %get-tuple-element.78.refs_0_, ...), custom_call_target="tpu_custom_call" | custom-call | tf_op jit(solution)/shard_map/place/pallas_call | solution.py:617
Async XLA Ops:
  0.6 2.1 %copy-start = (f32[4,512]{1,0:T(4,128)S(1)}, f32[4,512]{1,0:T(4,128)}, u32[]{:S(2)}) copy-start(f32[4,512]{1,0:T(4,128)} %param.16) | copy-start | bytes 24580
  2.7 0.7 copy-start.1

commit v4 on v3

--- a/solution.py
+++ b/solution.py
@@ -20,7 +20,7 @@
 IN_VMEM = pl.BlockSpec(memory_space=pltpu.VMEM)
 IN_SMEM = pl.BlockSpec(memory_space=pltpu.SMEM)
 ANYWHERE = pl.BlockSpec(memory_space=pl.ANY)
-VMEM_LIMIT = 62 * 1024 * 1024
+VMEM_LIMIT = 60 * 1024 * 1024
 
 
 def dot_nn(a, b):
@@ -85,7 +85,7 @@
     count, limit, heads, nblocks,
     doc, lq, lk, lv, ld, dec_in, aq, ado, att_k, att_v,
     lin_dq, lin_dk, lin_dv, att_dq, att_dk, att_dv,
-    wide, raw, dec, q, dout, kall, vall, parts, states, local, grads, mixed,
+    wide, raw, dec, q, dout, kall, vall, parts, states, local, grads,
     scores, probs_grad, peaks, top_ref, amount_ref, weighted_ref, dq_sum, flipped, dkey, dvalue,
     snd, got, paired, out, inbox,
     raw_sem, kv_send, kv_recv, pair_send, pair_recv, st_send, st_recv,
@@ -283,6 +283,10 @@
         state_write(0, side, totals[side], mults[side])
 
     state_start(0, 1)
+
+    @pl.when(jnp.logical_not(in_first))
+    def _():
+        state_start(0, 0)
 
     def state_join(side):
         state_wait(0, side)
@@ -463,7 +467,11 @@
             ref[...] = more[i]
 
     state_join(1)
-    state_start(0, 0)
+
+    @pl.when(in_first)
+    def _():
+        state_start(0, 0)
+
 
     stats = ready(tuple(ref[...] for ref in carry))
     acc = grade(0, 0, (0,), stats, jnp.zeros((width, chunk), F32))
@@ -511,12 +519,12 @@
     for side in range(2):
         state_wait(1, side)
 
+    intos, backs = [], []
     for h in range(heads):
         ends = []
         for side in range(2):
             close, mult = state_read(1, side, 0, h)
-            state = close + mult * state_read(1, side, 1, h)[0]
-            ends.append(state)
+            ends.append(close + mult * state_read(1, side, 1, h)[0])
         keep = [jnp.exp(head_terms(b, h)[2]) for b in range(nblocks)]
         state = ends[0]
         into = []
@@ -528,26 +536,20 @@
         for b in reversed(range(nblocks)):
             back[b] = precedes[b] * state
             state = states[1, b, h] + keep[b] * back[b]
-        for b in range(nblocks):
+        intos.append([x.astype(BF16) for x in into])
+        backs.append([x.astype(BF16) for x in back])
+    for b in range(nblocks):
+        for h in range(heads):
             row, col, total = head_terms(b, h)
             query, key, value, dol = (parts[a, b, h] for a in range(4))
             head_decay = jnp.exp(col)
             tail_decay = jnp.exp(total - col)
-            into_high, into_low = split(into[b])
-            back_high, back_low = split(back[b])
-            at = pl.ds(b * rows + h, TILE, stride=heads)
-            mixed[0, at, :] = grads[0, b, h] + head_decay * (
-                dot_nt(dol, into_high) + dot_nt(dol, into_low)
-            )
-            mixed[1, at, :] = grads[1, b, h] + tail_decay * (
-                dot_nt(value, back_high) + dot_nt(value, back_low)
-            )
-            mixed[2, at, :] = grads[2, b, h] + tail_decay * (
-                dot_nn(key, back_high) + dot_nn(key, back_low)
-            )
-    lin_dq[...] = mixed[0].astype(BF16)
-    lin_dk[...] = mixed[1].astype(BF16)
-    lin_dv[...] = mixed[2].astype(BF16)
+            at = pl.ds(h, TILE, stride=heads)
+            wide[0, at, :] = grads[0, b, h] + head_decay * dot_nt(dol, intos[h][b])
+            wide[1, at, :] = grads[1, b, h] + tail_decay * dot_nt(value, backs[h][b])
+            wide[2, at, :] = grads[2, b, h] + tail_decay * dot_nn(key, backs[h][b])
+        for a, ref in enumerate((lin_dq, lin_dk, lin_dv)):
+            ref[b * rows : (b + 1) * rows, :] = wide[a].astype(BF16)
 
     for which in range(2):
         grad_copy(which, 0).wait_recv()
@@ -647,7 +649,6 @@
             pltpu.VMEM((2, nblocks, heads, width, width), F32),
             pltpu.VMEM((2, heads, width, width), F32),
             pltpu.VMEM((3, nblocks, heads, TILE, width), F32),
-            pltpu.VMEM((3, rows, width), F32),
             pltpu.VMEM((held, TILE, TILE * heads), F32),
             pltpu.VMEM((held, TILE, TILE * heads), F32),
             pltpu.VMEM((nblocks, reach + 1, 1, TILE * heads), F32),

time: 68 us -> 51.5 us (0.76)
  Pallas kernels: 64.1 us -> 47.6 us
    pallas_call x1, Pallas kernels: 17 us -> 1.4 us  [place(): pl.pallas_call(place_kernel, out_shape=[SHAPE(x.shape, x.dtype) for x in...]
    pallas_call x1, Pallas kernels: 47 us -> 46.2 us  [call_whole(): pl.pallas_call(functools.partial(whole_kernel, count, limit, heads, nbloc...]
where the time goes in v4:
time: 51.5 us; the launch traced here: 51.4 us
  Pallas kernels  47.6 us (92%)
  between operations  1.48 us (3%)
  other arithmetic  1.44 us (3%)
  local copies, waits for them, and re-layouts  0.64 us (1%)
    pallas_call x1, Pallas kernels, call_whole(): pl.pallas_call(functools.partial(whole_kernel, count, limit, heads, nbloc...  46.2 us
    reduce_or x1, other arithmetic, shards(): long = jnp.any(later[SHORT:] == later[:-SHORT])  1.44 us
    pallas_call x1, Pallas kernels, place(): pl.pallas_call(place_kernel, out_shape=[SHAPE(x.shape, x.dtype) for x in...  1.4 us

profile of v4, /device:TPU:6, one launch (start us, length us, event | category | flops | bytes accessed | tf_op | source)
XLA Modules:
  0.0 51.4 jit_solution(3561779744309900598)
XLA Ops:
  0.6 0.0 copy-start
  0.6 1.4 %compare_reduce_fusion = pred[]{:T(512)} fusion(s32[32]{0:T(128)} %param.21), kind=kLoop, calls=%fused_computation | loop fusion | flops 23 | bytes 97 | tf_op jit(solution)/shard_map/reduce_or | solution.py:698
  2.7 0.0 copy-start.1
  2.7 0.0 copy-done
  2.8 0.6 %copy-done.1 = s32[32]{0:T(128)S(1)} copy-done((s32[32]{0:T(128)S(1)}, s32[32]{0:T(128)}, u32[]{:S(2)}) %copy-start.1) | copy-done | bytes 152
  3.4 46.4 %conditional.1 = ((bf16[2048,128]{1,0:T(8,128)(2,1)S(1)}, bf16[2048,128]{1,0:T(8,128)(2,1)S(1)}, bf16[2048,128]{1,0:T(8,128)(2,1)S(1)}, bf16[2048,128]{1,0:T(8,1...) conditional(s32[]{:T(128)} %convert_element_type.3, (s32[32]{0:T(128)S(1)}, ...), branch_computations={%region_1.0_spmd, %region_2.0_spmd} | conditional | bytes 8 | solution.py:699
  3.4 46.2 %whole_8.1 = (bf16[2048,128]{1,0:T(8,128)(2,1)S(1)}, bf16[2048,128]{1,0:T(8,128)(2,1)S(1)}, bf16[2048,128]{1,0:T(8,128)(2,1)S(1)}, bf16[2048,128]{1,0:T(8,128)(2...) custom-call(s32[32]{0:T(128)S(1)} %get-tuple-element.40.doc, ...), custom_call_target="tpu_custom_call" | custom-call | tf_op jit(solution)/shard_map/cond/branch_0_fun/whole_8/pallas_call | solution.py:635
  49.8 1.4 %place.1 = (bf16[2048,128]{1,0:T(8,128)(2,1)}, bf16[2048,128]{1,0:T(8,128)(2,1)}, bf16[2048,128]{1,0:T(8,128)(2,1)}, bf16[2048,128]{1,0:T(8,128)(2,1)}, bf16[256...) custom-call(bf16[2048,128]{1,0:T(8,128)(2,1)S(1)} %get-tuple-element.78.refs_0_, ...), custom_call_target="tpu_custom_call" | custom-call | tf_op jit(solution)/shard_map/place/pallas_call | solution.py:619
Async XLA Ops:
  0.6 2.1 %copy-start = (f32[4,512]{1,0:T(4,128)S(1)}, f32[4,512]{1,0:T(4,128)}, u32[]{:S(2)}) copy-start(f32[4,512]{1,0:T(4,128)} %param.16) | copy-start | bytes 24580
  2.7 0.7 %copy-start.1 = (s32[32]{0:T(128)S(1)}, s32[32]{0:T(128)}, u32[]{:S(2)}) copy-start(s32[32]{0:T(128)} %param.21) | copy-start | bytes 388

commit v5 on v4

--- a/solution.py
+++ b/solution.py
@@ -86,7 +86,7 @@
     doc, lq, lk, lv, ld, dec_in, aq, ado, att_k, att_v,
     lin_dq, lin_dk, lin_dv, att_dq, att_dk, att_dv,
     wide, raw, dec, q, dout, kall, vall, parts, states, local, grads,
-    scores, probs_grad, peaks, top_ref, amount_ref, weighted_ref, dq_sum, flipped, dkey, dvalue,
+    scores, probs_grad, peaks, top_ref, amount_ref, weighted_ref, middle, dq_sum, flipped, dkey, dvalue,
     snd, got, paired, out, inbox,
     raw_sem, kv_send, kv_recv, pair_send, pair_recv, st_send, st_recv,
     pg_send, pg_recv, home_send, home_recv,
@@ -249,12 +249,12 @@
 
     for b in range(nblocks):
         for a in range(4):
-            wide[a] = raw[a, b * rows : (b + 1) * rows, :].astype(F32)
+            wide[a % 3] = raw[a, b * rows : (b + 1) * rows, :].astype(F32)
+            for h in range(heads):
+                parts[a, b, h] = wide[a % 3, pl.ds(h, TILE, stride=heads), :].astype(BF16)
         for h in range(heads):
             row, col, total = head_terms(b, h)
-            picked = [wide[a, pl.ds(h, TILE, stride=heads), :] for a in range(4)]
-            for a in range(4):
-                parts[a, b, h] = picked[a].astype(BF16)
+            picked = [parts[a, b, h].astype(F32) for a in range(4)]
             key_high, key_low = split((picked[1] * jnp.exp(total - col)).T)
             value = picked[2].astype(BF16)
             states[0, b, h] = dot_nn(key_high, value) + dot_nn(key_low, value)
@@ -360,8 +360,8 @@
     far_tile = (reach - later_reach) * nblocks + 1
     queries = [q[b * chunk : (b + 1) * chunk, :] for b in range(nblocks)]
     douts = [dout[b * chunk : (b + 1) * chunk, :] for b in range(nblocks)]
-    dkey[rows_of(base + 1), :] = jnp.zeros((TILE, width), F32)
-    dvalue[rows_of(base + 1), :] = jnp.zeros((TILE, width), F32)
+    scores[0, base + 1 - offset] = jnp.zeros((TILE, chunk), BF16)
+    probs_grad[0, base + 1 - offset] = jnp.zeros((TILE, chunk), BF16)
 
     def keys_at(j, n):
         return pl.ds(pl.multiple_of(j * TILE, TILE), n * TILE)
@@ -403,37 +403,35 @@
         for k in range(len(tiles)):
             p = jnp.exp2(parts_s[k] - (peak + shades[k]))
             gk = g[k * TILE : (k + 1) * TILE]
-            scores[first + k - offset] = p
-            probs_grad[first + k - offset] = gk
+            scores[b, first + k - offset] = p.astype(BF16)
             amount += folded(p, jnp.sum)
             weighted += folded(p * gk, jnp.sum)
+        if diag:
+            middle[b] = jnp.sum(weighted, axis=0, keepdims=True) / jnp.sum(
+                amount, axis=0, keepdims=True
+            )
+        mid = middle[b]
+        for k in range(len(tiles)):
+            gk = g[k * TILE : (k + 1) * TILE]
+            probs_grad[b, first + k - offset] = (gk - mid).astype(BF16)
         peaks[b, step] = peak
         return peak, amount, weighted
 
-    def ready(carried):
+    def ready(b, carried):
         top, amount, weighted = carried
         inverse = 1.0 / jnp.sum(amount, axis=0, keepdims=True)
         delta = jnp.sum(weighted, axis=0, keepdims=True) * inverse
-        return top, inverse, delta
-
-    def grade(b, step, tiles, stats, acc):
+        return top, inverse, delta - middle[b]
+
+    def grade(b, step, tiles, stats):
         top, inverse, delta = stats
         first = (reach - step) * nblocks + tiles[0]
-        low = tiles[0] * TILE
         size = len(tiles) * TILE
         held = pl.ds(first - offset, len(tiles))
-        p = scores[held].reshape(size, chunk) * (jnp.exp2(peaks[b, step] - top) * inverse)
-        g = p * (probs_grad[held].reshape(size, chunk) - delta)
-        p = p.astype(BF16)
-        g = g.astype(BF16)
-        at = keys_at(first, len(tiles))
-        if b == 0:
-            dvalue[at, :] = dot_nn(p, douts[b])
-            dkey[at, :] = dot_nn(g, queries[b])
-        else:
-            dvalue[at, :] += dot_nn(p, douts[b])
-            dkey[at, :] += dot_nn(g, queries[b])
-        return acc + dot_nn(flipped[step, :, low : low + size], g)
+        p = scores[b, held].reshape(size, chunk).astype(F32)
+        p = p * (jnp.exp2(peaks[b, step] - top) * inverse)
+        g = p * (probs_grad[b, held].reshape(size, chunk).astype(F32) - delta)
+        return p.astype(BF16), g.astype(BF16)
 
     def finish(b, acc):
         att_dq[b * chunk : (b + 1) * chunk, :] = (acc.T * scale).astype(BF16)
@@ -441,19 +439,22 @@
     flip(0, (0, 1))
     row = jnp.zeros((8, chunk), F32)
     start = (jnp.full((1, chunk), NEG, F32), row, row)
-    state_zero = weigh(0, 0, (0,), start, diag=True)
-    for i, ref in enumerate(carry):
-        ref[...] = state_zero[i]
 
     def first_pass(step, carried):
         pass_on(step + 1)
         pair_wait(step)
         flip(step, (0, 1))
-        return weigh(0, step, (0, 1), carried)
-
-    carried = lax.fori_loop(1, near + 1, first_pass, state_zero)
+        return tuple(weigh(b, step, (0, 1), carried[b]) for b in range(nblocks))
+
+    carried = (weigh(0, 0, (0,), start, diag=True), weigh(1, 0, (0, 1), start, diag=True))
+
+    @pl.when(nright <= 0)
+    def _():
+        state_join(1)
+
+    carried = lax.fori_loop(1, near + 1, first_pass, carried)
     for i, ref in enumerate(carry):
-        ref[...] = carried[i]
+        ref[...] = carried[0][i]
 
     @pl.when(far)
     def _():
@@ -466,56 +467,60 @@
         for i, ref in enumerate(carry):
             ref[...] = more[i]
 
-    state_join(1)
+    @pl.when(nright > 0)
+    def _():
+        state_join(1)
 
     @pl.when(in_first)
     def _():
         state_start(0, 0)
 
-
-    stats = ready(tuple(ref[...] for ref in carry))
-    acc = grade(0, 0, (0,), stats, jnp.zeros((width, chunk), F32))
-    carried = weigh(1, 0, (0, 1), start, diag=True)
-
-    def both(step, packed):
-        carried, acc = packed
-        acc = grade(0, step, (0, 1), stats, acc)
-        return weigh(1, step, (0, 1), carried), acc
-
-    carried, acc = lax.fori_loop(1, near + 1, both, (carried, acc))
-    dq_sum[...] = acc
+    @pl.when(jnp.logical_not(in_first))
+    def _():
+        state_join(0)
+
+    stats = (ready(0, tuple(ref[...] for ref in carry)), ready(1, carried[1]))
+    dq_sum[...] = jnp.zeros((width, chunk), F32)
 
     @pl.when(far)
     def _():
-        dq_sum[...] = grade(0, later_reach, (1,), stats, dq_sum[...])
+        at = keys_at(far_tile, 1)
+        p, g = grade(0, later_reach, (1,), stats[0])
+        dkey[at, :] = dot_nn(g, queries[0])
+        dvalue[at, :] = dot_nn(p, douts[0])
+        dq_sum[...] = dot_nn(flipped[later_reach, :, TILE : 2 * TILE], g)
 
         @pl.when(core == 0)
         def _():
             for which in range(2):
                 grad_copy(which, later_reach).start()
 
-    finish(0, dq_sum[...])
-    state_join(0)
-
-    @pl.when(jnp.logical_and(far, core == 1))
-    def _():
-        send_home(later_reach)
-
-    last_stats = ready(carried)
-
     def last_pass(i, acc):
         step = near - i
-        acc = grade(1, step, (0, 1), last_stats, acc)
+        at = keys_at((reach - step) * nblocks, nblocks)
+        ones = [grade(b, step, (0, 1), stats[b]) for b in range(nblocks)]
+        p = jnp.concatenate([one[0] for one in ones], axis=1)
+        g = jnp.concatenate([one[1] for one in ones], axis=1)
+        dkey[at, :] = dot_nn(g, q[...])
+        dvalue[at, :] = dot_nn(p, dout[...])
         for which in range(2):
             grad_copy(which, step).start()
 
-        @pl.when(i > 0)
+        @pl.when(jnp.logical_or(i > 0, jnp.logical_and(far, core == 1)))
         def _():
             send_home(step + 1)
 
-        return acc
-
-    finish(1, lax.fori_loop(0, near + 1, last_pass, jnp.zeros((width, chunk), F32)))
+        return acc + dot_nn(flipped[step], g)
+
+    acc = jnp.concatenate([dq_sum[...], jnp.zeros((width, chunk), F32)], axis=1)
+    acc = lax.fori_loop(0, near + 1, last_pass, acc)
+    for b in range(nblocks):
+        finish(b, acc[:, b * chunk : (b + 1) * chunk])
+
+    @pl.when(in_first)
+    def _():
+        state_join(0)
+
     for side in range(2):
         state_wait(1, side)
 
@@ -595,6 +600,520 @@
                 grad_copy(which, step).wait_send()
 
 
+def long_kernel(
+    count, limit, heads, nblocks,
+    doc, lq, lk, lv, ld, dec_in, aq, ado, att_k, att_v,
+    lin_dq, lin_dk, lin_dv, att_dq, att_dk, att_dv,
+    wide, raw, dec, q, dout, kall, vall, parts, states, local, grads,
+    scores, probs_grad, peaks, top_ref, amount_ref, weighted_ref, dq_sum, flipped, dkey, dvalue,
+    snd, got, paired, out, inbox,
+    raw_sem, kv_send, kv_recv, pair_send, pair_recv, st_send, st_recv,
+    pg_send, pg_recv, home_send, home_recv,
+):
+    me = lax.axis_index("ctx")
+    carry = (top_ref, amount_ref, weighted_ref)
+    core = lax.axis_index("head")
+    length = nblocks * TILE
+    width = lq.shape[1]
+    rows = TILE * heads
+    first_devs = MOST // nblocks
+    in_first = me < first_devs
+    later_reach = limit // nblocks
+    reach = slots_of(limit, nblocks)
+    most = jnp.where(in_first, first_devs - 1, later_reach)
+    nleft = jnp.minimum(jnp.where(in_first, me, me - first_devs), most)
+    nright = jnp.minimum(jnp.where(in_first, first_devs - 1 - me, count - 1 - me), most)
+    span = jnp.where(in_first, MOST, limit)
+
+    def takes(step, there, who):
+        if isinstance(step, int) and step != later_reach:
+            return step <= there
+        far = jnp.logical_and(step == later_reach, jnp.logical_not(in_first))
+        return jnp.logical_and(step <= there, jnp.logical_or(jnp.logical_not(far), core == who))
+
+    scale = width ** (-0.5)
+    factor = scale * math.log2(math.e)
+
+    loads = [
+        pltpu.make_async_copy(ref, raw.at[a], raw_sem.at[a])
+        for a, ref in enumerate((lq, lk, lv, ld))
+    ]
+    loads.append(pltpu.make_async_copy(dec_in, dec, raw_sem.at[4]))
+    loads.append(pltpu.make_async_copy(aq, q, raw_sem.at[5]))
+    loads.append(pltpu.make_async_copy(ado, dout, raw_sem.at[6]))
+    own_rows = pl.ds(reach * length, length)
+    loads.append(pltpu.make_async_copy(att_k, kall.at[own_rows], raw_sem.at[7]))
+    loads.append(pltpu.make_async_copy(att_v, vall.at[own_rows], raw_sem.at[8]))
+    for load in loads:
+        load.start()
+
+    barrier = pltpu.get_barrier_semaphore()
+    pl.semaphore_signal(barrier, inc=1, device_id={"head": 1 - core}, device_id_type=MESH)
+    for step in range(1, reach + 1):
+
+        @pl.when(step <= nright)
+        def _():
+            pl.semaphore_signal(barrier, inc=1, device_id={"ctx": me + step}, device_id_type=MESH)
+
+        @pl.when(step <= nleft)
+        def _():
+            pl.semaphore_signal(barrier, inc=1, device_id={"ctx": me - step}, device_id_type=MESH)
+
+    pl.semaphore_wait(barrier, 1 + nleft + nright)
+
+    pairs = ((att_k, kall), (att_v, vall))
+
+    def half_of(step):
+        start = pl.multiple_of(core * TILE, TILE)
+        return start, pl.ds((reach - step) * length + start, TILE)
+
+    def kv_copy(which, step):
+        start, place = half_of(step)
+        source, target = pairs[which]
+        return pltpu.make_async_remote_copy(
+            src_ref=source.at[pl.ds(start, TILE)],
+            dst_ref=target.at[place],
+            send_sem=kv_send.at[which, step - 1],
+            recv_sem=kv_recv.at[which, step - 1],
+            device_id={"ctx": me + step},
+            device_id_type=MESH,
+        )
+
+    def pair_copy(which, step):
+        target = pairs[which][1]
+        place = half_of(step)[1]
+        return pltpu.make_async_remote_copy(
+            src_ref=target.at[place],
+            dst_ref=target.at[place],
+            send_sem=pair_send.at[which, step - 1],
+            recv_sem=pair_recv.at[which, step - 1],
+            device_id={"head": 1 - core},
+            device_id_type=MESH,
+        )
+
+    def pass_on(step):
+        @pl.when(takes(step, nleft, 1))
+        def _():
+            for which in range(2):
+                kv_copy(which, step).wait_recv()
+                pair_copy(which, step).start()
+
+    def pair_wait(step):
+        for which in range(2):
+            pair_copy(which, step).wait_recv()
+
+    hops = ((1, 2), (1, 4))
+
+    def state_copy(trip, side, k):
+        hop = hops[trip][k]
+        return pltpu.make_async_remote_copy(
+            src_ref=snd.at[trip, side],
+            dst_ref=got.at[trip, side, k],
+            send_sem=st_send.at[trip, side, k],
+            recv_sem=st_recv.at[trip, side, k],
+            device_id={"ctx": me + hop if side == 0 else me - hop},
+            device_id_type=MESH,
+        )
+
+    def sent(side):
+        return nright if side == 0 else nleft
+
+    def due(side):
+        return nleft if side == 0 else nright
+
+    def state_start(trip, side):
+        for k, hop in enumerate(hops[trip]):
+
+            @pl.when(hop <= sent(side))
+            def _():
+                state_copy(trip, side, k).start()
+
+            @pl.when(hop > due(side))
+            def _():
+                got[trip, side, k] = jnp.zeros(got.shape[3:], BF16)
+
+    def state_wait(trip, side):
+        for k, hop in enumerate(hops[trip]):
+
+            @pl.when(hop <= due(side))
+            def _():
+                state_copy(trip, side, k).wait_recv()
+
+    def state_write(trip, side, totals, mults):
+        pads = []
+        for h in range(heads):
+            snd[trip, side, h * width : (h + 1) * width, :] = totals[h].astype(BF16)
+            high, low = split(jnp.broadcast_to(mults[h], (1, width)))
+            pads.append((high.astype(F32), low.astype(F32)))
+        rows16 = [pads[h][0] for h in range(heads)] + [pads[h][1] for h in range(heads)]
+        rows16.append(jnp.zeros((16 - 2 * heads, width), F32))
+        snd[trip, side, heads * width :, :] = jnp.concatenate(rows16, axis=0).astype(BF16)
+
+    def state_read(trip, side, k, h):
+        at = heads * width
+        total = got[trip, side, k, h * width : (h + 1) * width, :].astype(F32)
+        pads = got[trip, side, k, at : at + 16, :].astype(F32)
+        return total, pads[h : h + 1] + pads[heads + h : heads + h + 1]
+
+    for step in range(1, reach + 1):
+
+        @pl.when(takes(step, nright, 1))
+        def _():
+            for which in range(2):
+                kv_copy(which, step).start()
+
+    for load in loads:
+        load.wait()
+    follows, precedes, head_terms, t_sub, t_lane = decay_terms(me, count, nblocks, doc, dec)
+
+    for b in range(nblocks):
+        for a in range(4):
+            wide[a] = raw[a, b * rows : (b + 1) * rows, :].astype(F32)
+        for h in range(heads):
+            row, col, total = head_terms(b, h)
+            picked = [wide[a, pl.ds(h, TILE, stride=heads), :] for a in range(4)]
+            for a in range(4):
+                parts[a, b, h] = picked[a].astype(BF16)
+            key_high, key_low = split((picked[1] * jnp.exp(total - col)).T)
+            value = picked[2].astype(BF16)
+            states[0, b, h] = dot_nn(key_high, value) + dot_nn(key_low, value)
+            query_high, query_low = split((picked[0] * jnp.exp(col)).T)
+            dol = picked[3].astype(BF16)
+            states[1, b, h] = dot_nn(query_high, dol) + dot_nn(query_low, dol)
+
+    totals, mults = ([], []), ([], [])
+    for h in range(heads):
+        keep = [jnp.exp(head_terms(b, h)[2]) for b in range(nblocks)]
+        total_l = states[0, 0, h]
+        mult_l = keep[0] * follows[0]
+        for b in range(1, nblocks):
+            total_l = states[0, b, h] + keep[b] * follows[b] * total_l
+            mult_l = mult_l * keep[b] * follows[b]
+        total_r = states[1, nblocks - 1, h]
+        mult_r = keep[nblocks - 1] * precedes[nblocks - 1]
+        for b in reversed(range(nblocks - 1)):
+            total_r = states[1, b, h] + keep[b] * precedes[b] * total_r
+            mult_r = mult_r * keep[b] * precedes[b]
+        for side, total, mult in ((0, total_l, mult_l), (1, total_r, mult_r)):
+            totals[side].append(total)
+            mults[side].append(mult)
+            local[side, h] = total
+    for side in range(2):
+        state_write(0, side, totals[side], mults[side])
+
+    state_start(0, 1)
+
+    @pl.when(jnp.logical_not(in_first))
+    def _():
+        state_start(0, 0)
+
+    def state_join(side):
+        state_wait(0, side)
+        joined, spans = [], []
+        for h in range(heads):
+            one, mult_one = state_read(0, side, 0, h)
+            two, mult_two = state_read(0, side, 1, h)
+            joined.append(local[side, h] + mults[side][h] * (one + mult_one * two))
+            spans.append(mults[side][h] * mult_one * mult_two)
+        state_write(1, side, joined, spans)
+        state_start(1, side)
+
+
+    def within(b):
+        for h in range(heads):
+            row, col, total = head_terms(b, h)
+            query, key, value, dol = (parts[a, b, h] for a in range(4))
+            seen = t_sub <= t_lane
+            weight = jnp.where(seen, jnp.exp(jnp.where(seen, row - col, 0.0)), 0.0)
+            left = (dot_nt(value, dol) * weight).astype(BF16)
+            right = (dot_nt(key, query) * weight).astype(BF16)
+            grads[0, b, h] = dot_tn(left, key)
+            grads[1, b, h] = dot_nn(left, query)
+            grads[2, b, h] = dot_nn(right, dol)
+
+    within(0)
+    pass_on(1)
+    for b in range(1, nblocks):
+        within(b)
+    def rows_of(j):
+        return pl.ds(pl.multiple_of(j * TILE, TILE), TILE)
+
+    sources = (dkey, dvalue)
+
+    def grad_copy(which, step):
+        return pltpu.make_async_remote_copy(
+            src_ref=sources[which].at[rows_of((reach - step) * nblocks + 1 - core)],
+            dst_ref=paired.at[which, step],
+            send_sem=pg_send.at[which, step],
+            recv_sem=pg_recv.at[which, step],
+            device_id={"head": 1 - core},
+            device_id_type=MESH,
+        )
+
+    def home_copy(step):
+        return pltpu.make_async_remote_copy(
+            src_ref=out.at[step - 1],
+            dst_ref=inbox.at[step - 1],
+            send_sem=home_send.at[step - 1],
+            recv_sem=home_recv.at[step - 1],
+            device_id={"ctx": me - step},
+            device_id_type=MESH,
+        )
+
+    def mine(which, step):
+        place = rows_of((reach - step) * nblocks + core)
+        return sources[which][place, :] + paired[which, step]
+
+    def send_home(step):
+        for which in range(2):
+            grad_copy(which, step).wait_recv()
+        for which in range(2):
+            out[step - 1, which] = mine(which, step).astype(BF16)
+        home_copy(step).start()
+
+    chunk = rows
+    base = reach * nblocks
+    offset = offset_of(limit, nblocks)
+    near = jnp.minimum(nleft, jnp.where(in_first, reach, later_reach - 1))
+    far = jnp.logical_and(jnp.logical_not(in_first), nleft == later_reach)
+    far_tile = (reach - later_reach) * nblocks + 1
+    queries = [q[b * chunk : (b + 1) * chunk, :] for b in range(nblocks)]
+    douts = [dout[b * chunk : (b + 1) * chunk, :] for b in range(nblocks)]
+    dkey[rows_of(base + 1), :] = jnp.zeros((TILE, width), F32)
+    dvalue[rows_of(base + 1), :] = jnp.zeros((TILE, width), F32)
+
+    def keys_at(j, n):
+        return pl.ds(pl.multiple_of(j * TILE, TILE), n * TILE)
+
+    def hidden(b, j):
+        at = jnp.clip(me * nblocks - base + j, 0, count * nblocks - 1)
+        return jnp.where(doc[at] == doc[me * nblocks + b], 0.0, -NEG).astype(F32)
+
+    def folded(x, op):
+        return op(x.reshape(TILE // 8, 8, chunk), axis=0)
+
+    def causal():
+        token = lax.broadcasted_iota(jnp.int32, (TILE, chunk), 1) // heads
+        return lax.broadcasted_iota(jnp.int32, (TILE, chunk), 0) <= token
+
+    def flip(step, tiles):
+        first = (reach - step) * nblocks + tiles[0]
+        low = tiles[0] * TILE
+        block = kall[keys_at(first, len(tiles)), :].astype(F32).T.astype(BF16)
+        flipped[step, :, low : low + len(tiles) * TILE] = block
+
+    def weigh(b, step, tiles, carried, diag=False):
+        top, amount, weighted = carried
+        first = (reach - step) * nblocks + tiles[0]
+        at = keys_at(first, len(tiles))
+        s = dot_nt(kall[at, :], queries[b]) * factor
+        g = dot_nt(vall[at, :], douts[b])
+        parts_s = [s[k * TILE : (k + 1) * TILE] for k in range(len(tiles))]
+        shades = [hidden(b, first + k) for k in range(len(tiles))]
+        if diag:
+            parts_s[-1] = jnp.where(causal(), parts_s[-1], NEG)
+        peak = folded(parts_s[0], jnp.max) - shades[0]
+        for k in range(1, len(tiles)):
+            peak = jnp.maximum(peak, folded(parts_s[k], jnp.max) - shades[k])
+        peak = jnp.maximum(top, jnp.max(peak, axis=0, keepdims=True))
+        shrink = jnp.exp2(top - peak)
+        amount = amount * shrink
+        weighted = weighted * shrink
+        for k in range(len(tiles)):
+            p = jnp.exp2(parts_s[k] - (peak + shades[k]))
+            gk = g[k * TILE : (k + 1) * TILE]
+            scores[first + k - offset] = p
+            probs_grad[first + k - offset] = gk
+            amount += folded(p, jnp.sum)
+            weighted += folded(p * gk, jnp.sum)
+        peaks[b, step] = peak
+        return peak, amount, weighted
+
+    def ready(carried):
+        top, amount, weighted = carried
+        inverse = 1.0 / jnp.sum(amount, axis=0, keepdims=True)
+        delta = jnp.sum(weighted, axis=0, keepdims=True) * inverse
+        return top, inverse, delta
+
+    def grade(b, step, tiles, stats, acc):
+        top, inverse, delta = stats
+        first = (reach - step) * nblocks + tiles[0]
+        low = tiles[0] * TILE
+        size = len(tiles) * TILE
+        held = pl.ds(first - offset, len(tiles))
+        p = scores[held].reshape(size, chunk) * (jnp.exp2(peaks[b, step] - top) * inverse)
+        g = p * (probs_grad[held].reshape(size, chunk) - delta)
+        p = p.astype(BF16)
+        g = g.astype(BF16)
+        at = keys_at(first, len(tiles))
+        if b == 0:
+            dvalue[at, :] = dot_nn(p, douts[b])
+            dkey[at, :] = dot_nn(g, queries[b])
+        else:
+            dvalue[at, :] += dot_nn(p, douts[b])
+            dkey[at, :] += dot_nn(g, queries[b])
+        return acc + dot_nn(flipped[step, :, low : low + size], g)
+
+    def finish(b, acc):
+        att_dq[b * chunk : (b + 1) * chunk, :] = (acc.T * scale).astype(BF16)
+
+    flip(0, (0, 1))
+    row = jnp.zeros((8, chunk), F32)
+    start = (jnp.full((1, chunk), NEG, F32), row, row)
+    state_zero = weigh(0, 0, (0,), start, diag=True)
+    for i, ref in enumerate(carry):
+        ref[...] = state_zero[i]
+
+    def first_pass(step, carried):
+        pass_on(step + 1)
+        pair_wait(step)
+        flip(step, (0, 1))
+        return weigh(0, step, (0, 1), carried)
+
+    carried = lax.fori_loop(1, near + 1, first_pass, state_zero)
+    for i, ref in enumerate(carry):
+        ref[...] = carried[i]
+
+    @pl.when(far)
+    def _():
+        @pl.when(core == 0)
+        def _():
+            pair_wait(later_reach)
+
+        flip(later_reach, (1,))
+        more = weigh(0, later_reach, (1,), tuple(ref[...] for ref in carry))
+        for i, ref in enumerate(carry):
+            ref[...] = more[i]
+
+    state_join(1)
+
+    @pl.when(in_first)
+    def _():
+        state_start(0, 0)
+
+
+    stats = ready(tuple(ref[...] for ref in carry))
+    acc = grade(0, 0, (0,), stats, jnp.zeros((width, chunk), F32))
+    carried = weigh(1, 0, (0, 1), start, diag=True)
+
+    def both(step, packed):
+        carried, acc = packed
+        acc = grade(0, step, (0, 1), stats, acc)
+        return weigh(1, step, (0, 1), carried), acc
+
+    carried, acc = lax.fori_loop(1, near + 1, both, (carried, acc))
+    dq_sum[...] = acc
+
+    @pl.when(far)
+    def _():
+        dq_sum[...] = grade(0, later_reach, (1,), stats, dq_sum[...])
+
+        @pl.when(core == 0)
+        def _():
+            for which in range(2):
+                grad_copy(which, later_reach).start()
+
+    finish(0, dq_sum[...])
+    state_join(0)
+
+    @pl.when(jnp.logical_and(far, core == 1))
+    def _():
+        send_home(later_reach)
+
+    last_stats = ready(carried)
+
+    def last_pass(i, acc):
+        step = near - i
+        acc = grade(1, step, (0, 1), last_stats, acc)
+        for which in range(2):
+            grad_copy(which, step).start()
+
+        @pl.when(i > 0)
+        def _():
+            send_home(step + 1)
+
+        return acc
+
+    finish(1, lax.fori_loop(0, near + 1, last_pass, jnp.zeros((width, chunk), F32)))
+    for side in range(2):
+        state_wait(1, side)
+
+    intos, backs = [], []
+    for h in range(heads):
+        ends = []
+        for side in range(2):
+            close, mult = state_read(1, side, 0, h)
+            ends.append(close + mult * state_read(1, side, 1, h)[0])
+        keep = [jnp.exp(head_terms(b, h)[2]) for b in range(nblocks)]
+        state = ends[0]
+        into = []
+        for b in range(nblocks):
+            into.append(follows[b] * state)
+            state = states[0, b, h] + keep[b] * into[b]
+        state = ends[1]
+        back = [None] * nblocks
+        for b in reversed(range(nblocks)):
+            back[b] = precedes[b] * state
+            state = states[1, b, h] + keep[b] * back[b]
+        intos.append([x.astype(BF16) for x in into])
+        backs.append([x.astype(BF16) for x in back])
+    for b in range(nblocks):
+        for h in range(heads):
+            row, col, total = head_terms(b, h)
+            query, key, value, dol = (parts[a, b, h] for a in range(4))
+            head_decay = jnp.exp(col)
+            tail_decay = jnp.exp(total - col)
+            at = pl.ds(h, TILE, stride=heads)
+            wide[0, at, :] = grads[0, b, h] + head_decay * dot_nt(dol, intos[h][b])
+            wide[1, at, :] = grads[1, b, h] + tail_decay * dot_nt(value, backs[h][b])
+            wide[2, at, :] = grads[2, b, h] + tail_decay * dot_nn(key, backs[h][b])
+        for a, ref in enumerate((lin_dq, lin_dk, lin_dv)):
+            ref[b * rows : (b + 1) * rows, :] = wide[a].astype(BF16)
+
+    for which in range(2):
+        grad_copy(which, 0).wait_recv()
+        paired[which, 0] = mine(which, 0)
+
+    for step in range(1, reach + 1):
+
+        @pl.when(takes(step, nright, 1))
+        def _():
+            home_copy(step).wait_recv()
+            for which in range(2):
+                paired[which, 0] += inbox[step - 1, which].astype(F32)
+
+    att_dk[...] = (paired[0, 0] * scale).astype(BF16)
+    att_dv[...] = paired[1, 0].astype(BF16)
+
+    for which in range(2):
+        grad_copy(which, 0).wait_send()
+    for trip in range(2):
+        for k, hop in enumerate(hops[trip]):
+            for side, there in ((0, nright), (1, nleft)):
+
+                @pl.when(hop <= there)
+                def _():
+                    state_copy(trip, side, k).wait_send()
+
+    for step in range(1, reach + 1):
+
+        @pl.when(takes(step, nright, 1))
+        def _():
+            for which in range(2):
+                kv_copy(which, step).wait_send()
+
+        @pl.when(takes(step, nleft, 1))
+        def _():
+            for which in range(2):
+                pair_copy(which, step).wait_send()
+            home_copy(step).wait_send()
+
+        @pl.when(takes(step, nleft, 0))
+        def _():
+            for which in range(2):
+                grad_copy(which, step).wait_send()
+
+
 def slots_of(limit, nblocks):
     return max(MOST // nblocks - 1, limit // nblocks)
 
@@ -634,6 +1153,66 @@
     held = (reach + 1) * nblocks - offset_of(limit, nblocks)
     return pl.pallas_call(
         functools.partial(whole_kernel, count, limit, heads, nblocks),
+        out_shape=[SHAPE((rows, width), BF16)] * 4 + [SHAPE((TILE, width), BF16)] * 2,
+        in_specs=[IN_SMEM] + [ANYWHERE] * 9,
+        out_specs=[IN_VMEM] * 6,
+        scratch_shapes=[
+            pltpu.VMEM((3, TILE * heads, width), F32),
+            pltpu.VMEM((4, rows, width), BF16),
+            pltpu.VMEM((heads, nblocks * TILE), F32),
+            pltpu.VMEM((rows, width), BF16),
+            pltpu.VMEM((rows, width), BF16),
+            pltpu.VMEM((window, width), BF16),
+            pltpu.VMEM((window, width), BF16),
+            pltpu.VMEM((4, nblocks, heads, TILE, width), BF16),
+            pltpu.VMEM((2, nblocks, heads, width, width), F32),
+            pltpu.VMEM((2, heads, width, width), F32),
+            pltpu.VMEM((3, nblocks, heads, TILE, width), F32),
+            pltpu.VMEM((nblocks, held, TILE, TILE * heads), BF16),
+            pltpu.VMEM((nblocks, held, TILE, TILE * heads), BF16),
+            pltpu.VMEM((nblocks, reach + 1, 1, TILE * heads), F32),
+            pltpu.VMEM((1, TILE * heads), F32),
+            pltpu.VMEM((8, TILE * heads), F32),
+            pltpu.VMEM((8, TILE * heads), F32),
+            pltpu.VMEM((nblocks, 1, TILE * heads), F32),
+            pltpu.VMEM((width, TILE * heads), F32),
+            pltpu.VMEM((reach + 1, width, nblocks * TILE), BF16),
+            pltpu.VMEM((window, width), F32),
+            pltpu.VMEM((window, width), F32),
+            pltpu.VMEM((2, 2, heads * width + 16, width), BF16),
+            pltpu.VMEM((2, 2, 2, heads * width + 16, width), BF16),
+            pltpu.VMEM((2, reach + 1, TILE, width), F32),
+            pltpu.VMEM((reach, 2, TILE, width), BF16),
+            pltpu.VMEM((reach, 2, TILE, width), BF16),
+            DMA((9,)),
+            DMA((2, reach)),
+            DMA((2, reach)),
+            DMA((2, reach)),
+            DMA((2, reach)),
+            DMA((2, 2, 2)),
+            DMA((2, 2, 2)),
+            DMA((2, reach + 1)),
+            DMA((2, reach + 1)),
+            DMA((reach,)),
+            DMA((reach,)),
+        ],
+        compiler_params=pltpu.CompilerParams(
+            collective_id=0 if limit == MOST else 1,
+            has_side_effects=True,
+            vmem_limit_bytes=VMEM_LIMIT,
+        ),
+        name="whole_%d" % limit,
+    )(*args)
+
+
+def call_long(count, limit, heads, nblocks, args):
+    width = args[-1].shape[1]
+    rows = nblocks * TILE * heads
+    reach = slots_of(limit, nblocks)
+    window = (reach + 1) * nblocks * TILE
+    held = (reach + 1) * nblocks - offset_of(limit, nblocks)
+    return pl.pallas_call(
+        functools.partial(long_kernel, count, limit, heads, nblocks),
         out_shape=[SHAPE((rows, width), BF16)] * 4 + [SHAPE((TILE, width), BF16)] * 2,
         in_specs=[IN_SMEM] + [ANYWHERE] * 9,
         out_specs=[IN_VMEM] * 6,
@@ -681,7 +1260,7 @@
             has_side_effects=True,
             vmem_limit_bytes=VMEM_LIMIT,
         ),
-        name="whole_%d" % limit,
+        name="long_%d" % limit,
     )(*args)
 
 
@@ -698,7 +1277,7 @@
     long = jnp.any(later[SHORT:] == later[:-SHORT])
     outs = lax.cond(
         long,
-        lambda *a: call_whole(count, MOST, heads, nblocks, a),
+        lambda *a: call_long(count, MOST, heads, nblocks, a),
         lambda *a: call_whole(count, SHORT, heads, nblocks, a),
         *args,
     )

time: 51.5 us -> 48.4 us (0.940)
  Pallas kernels: 47.6 us -> 44.5 us
    pallas_call x1, Pallas kernels: 46.2 us -> 43.1 us  [call_whole(): pl.pallas_call(functools.partial(whole_kernel, count, limit, heads, nbloc...]
where the time goes in v5:
time: 48.4 us; the launch traced here: 48.2 us
  Pallas kernels  44.5 us (92%)
  between operations  1.48 us (3%)
  other arithmetic  1.44 us (3%)
  local copies, waits for them, and re-layouts  0.64 us (1%)
    pallas_call x1, Pallas kernels, call_whole(): pl.pallas_call(functools.partial(whole_kernel, count, limit, heads, nbloc...  43.1 us
    reduce_or x1, other arithmetic, shards(): long = jnp.any(later[SHORT:] == later[:-SHORT])  1.44 us
    pallas_call x1, Pallas kernels, place(): pl.pallas_call(place_kernel, out_shape=[SHAPE(x.shape, x.dtype) for x in...  1.4 us

profile of v5, /device:TPU:6, one launch (start us, length us, event | category | flops | bytes accessed | tf_op | source)
XLA Modules:
  0.0 48.2 jit_solution(4303181674753336146)
XLA Ops:
  0.6 0.0 copy-start
  0.6 1.4 %compare_reduce_fusion = pred[]{:T(512)} fusion(s32[32]{0:T(128)} %param.21), kind=kLoop, calls=%fused_computation | loop fusion | flops 23 | bytes 97 | tf_op jit(solution)/shard_map/reduce_or | solution.py:1277
  2.7 0.0 copy-start.1
  2.7 0.0 copy-done
  2.8 0.6 %copy-done.1 = s32[32]{0:T(128)S(1)} copy-done((s32[32]{0:T(128)S(1)}, s32[32]{0:T(128)}, u32[]{:S(2)}) %copy-start.1) | copy-done | bytes 152
  3.4 43.3 %conditional.1 = ((bf16[2048,128]{1,0:T(8,128)(2,1)S(1)}, bf16[2048,128]{1,0:T(8,128)(2,1)S(1)}, bf16[2048,128]{1,0:T(8,128)(2,1)S(1)}, bf16[2048,128]{1,0:T(8,1...) conditional(s32[]{:T(128)} %convert_element_type.3, (s32[32]{0:T(128)S(1)}, ...), branch_computations={%region_1.0_spmd, %region_2.0_spmd} | conditional | bytes 8 | solution.py:1278
  3.4 43.1 %whole_8.1 = (bf16[2048,128]{1,0:T(8,128)(2,1)S(1)}, bf16[2048,128]{1,0:T(8,128)(2,1)S(1)}, bf16[2048,128]{1,0:T(8,128)(2,1)S(1)}, bf16[2048,128]{1,0:T(8,128)(2...) custom-call(s32[32]{0:T(128)S(1)} %get-tuple-element.40.doc, ...), custom_call_target="tpu_custom_call" | custom-call | tf_op jit(solution)/shard_map/cond/branch_0_fun/whole_8/pallas_call | solution.py:1154
  46.7 1.4 %place.1 = (bf16[2048,128]{1,0:T(8,128)(2,1)}, bf16[2048,128]{1,0:T(8,128)(2,1)}, bf16[2048,128]{1,0:T(8,128)(2,1)}, bf16[2048,128]{1,0:T(8,128)(2,1)}, bf16[256...) custom-call(bf16[2048,128]{1,0:T(8,128)(2,1)S(1)} %get-tuple-element.78.refs_0_, ...), custom_call_target="tpu_custom_call" | custom-call | tf_op jit(solution)/shard_map/place/pallas_call | solution.py:1138
Async XLA Ops:
  0.6 2.1 %copy-start = (f32[4,512]{1,0:T(4,128)S(1)}, f32[4,512]{1,0:T(4,128)}, u32[]{:S(2)}) copy-start(f32[4,512]{1,0:T(4,128)} %param.16) | copy-start | bytes 24580
  2.7 0.7 %copy-start.1 = (s32[32]{0:T(128)S(1)}, s32[32]{0:T(128)}, u32[]{:S(2)}) copy-start(s32[32]{0:T(128)} %param.21) | copy-start | bytes 388

commit v6 on v5

--- a/solution.py
+++ b/solution.py
@@ -383,12 +383,12 @@
         block = kall[keys_at(first, len(tiles)), :].astype(F32).T.astype(BF16)
         flipped[step, :, low : low + len(tiles) * TILE] = block
 
-    def weigh(b, step, tiles, carried, diag=False):
+    def weigh(b, step, tiles, carried, diag=False, given=None):
         top, amount, weighted = carried
         first = (reach - step) * nblocks + tiles[0]
         at = keys_at(first, len(tiles))
-        s = dot_nt(kall[at, :], queries[b]) * factor
-        g = dot_nt(vall[at, :], douts[b])
+        s, g = given or (dot_nt(kall[at, :], queries[b]), dot_nt(vall[at, :], douts[b]))
+        s = s * factor
         parts_s = [s[k * TILE : (k + 1) * TILE] for k in range(len(tiles))]
         shades = [hidden(b, first + k) for k in range(len(tiles))]
         if diag:
@@ -444,7 +444,14 @@
         pass_on(step + 1)
         pair_wait(step)
         flip(step, (0, 1))
-        return tuple(weigh(b, step, (0, 1), carried[b]) for b in range(nblocks))
+        at = keys_at((reach - step) * nblocks, nblocks)
+        s = dot_nt(kall[at, :], q[...])
+        g = dot_nt(vall[at, :], dout[...])
+        cuts = [slice(b * chunk, (b + 1) * chunk) for b in range(nblocks)]
+        return tuple(
+            weigh(b, step, (0, 1), carried[b], given=(s[:, cuts[b]], g[:, cuts[b]]))
+            for b in range(nblocks)
+        )
 
     carried = (weigh(0, 0, (0,), start, diag=True), weigh(1, 0, (0, 1), start, diag=True))
 

time: 48.4 us -> 48.2 us (level)
  no operation moved by 1% of the time
where the time goes in v6:
time: 48.2 us; the launch traced here: 48 us
  Pallas kernels  44.3 us (92%)
  between operations  1.48 us (3%)
  other arithmetic  1.44 us (3%)
  local copies, waits for them, and re-layouts  0.64 us (1%)
    pallas_call x1, Pallas kernels, call_whole(): pl.pallas_call(functools.partial(whole_kernel, count, limit, heads, nbloc...  42.9 us
    reduce_or x1, other arithmetic, shards(): long = jnp.any(later[SHORT:] == later[:-SHORT])  1.44 us
    pallas_call x1, Pallas kernels, place(): pl.pallas_call(place_kernel, out_shape=[SHAPE(x.shape, x.dtype) for x in...  1.4 us

profile of v6, /device:TPU:6, one launch (start us, length us, event | category | flops | bytes accessed | tf_op | source)
XLA Modules:
  0.0 48.0 jit_solution(3859568999507962023)
XLA Ops:
  0.6 0.0 copy-start
  0.6 1.4 %compare_reduce_fusion = pred[]{:T(512)} fusion(s32[32]{0:T(128)} %param.21), kind=kLoop, calls=%fused_computation | loop fusion | flops 23 | bytes 97 | tf_op jit(solution)/shard_map/reduce_or | solution.py:1284
  2.7 0.0 copy-start.1
  2.7 0.0 copy-done
  2.8 0.6 %copy-done.1 = s32[32]{0:T(128)S(1)} copy-done((s32[32]{0:T(128)S(1)}, s32[32]{0:T(128)}, u32[]{:S(2)}) %copy-start.1) | copy-done | bytes 152
  3.4 43.1 %conditional.1 = ((bf16[2048,128]{1,0:T(8,128)(2,1)S(1)}, bf16[2048,128]{1,0:T(8,128)(2,1)S(1)}, bf16[2048,128]{1,0:T(8,128)(2,1)S(1)}, bf16[2048,128]{1,0:T(8,1...) conditional(s32[]{:T(128)} %convert_element_type.3, (s32[32]{0:T(128)S(1)}, ...), branch_computations={%region_1.0_spmd, %region_2.0_spmd} | conditional | bytes 8 | solution.py:1285
  3.4 42.9 %whole_8.1 = (bf16[2048,128]{1,0:T(8,128)(2,1)S(1)}, bf16[2048,128]{1,0:T(8,128)(2,1)S(1)}, bf16[2048,128]{1,0:T(8,128)(2,1)S(1)}, bf16[2048,128]{1,0:T(8,128)(2...) custom-call(s32[32]{0:T(128)S(1)} %get-tuple-element.40.doc, ...), custom_call_target="tpu_custom_call" | custom-call | tf_op jit(solution)/shard_map/cond/branch_0_fun/whole_8/pallas_call | solution.py:1161
  46.5 1.4 %place.1 = (bf16[2048,128]{1,0:T(8,128)(2,1)}, bf16[2048,128]{1,0:T(8,128)(2,1)}, bf16[2048,128]{1,0:T(8,128)(2,1)}, bf16[2048,128]{1,0:T(8,128)(2,1)}, bf16[256...) custom-call(bf16[2048,128]{1,0:T(8,128)(2,1)S(1)} %get-tuple-element.78.refs_0_, ...), custom_call_target="tpu_custom_call" | custom-call | tf_op jit(solution)/shard_map/place/pallas_call | solution.py:1145
Async XLA Ops:
  0.6 2.1 %copy-start = (f32[4,512]{1,0:T(4,128)S(1)}, f32[4,512]{1,0:T(4,128)}, u32[]{:S(2)}) copy-start(f32[4,512]{1,0:T(4,128)} %param.16) | copy-start | bytes 24580
  2.7 0.7 %copy-start.1 = (s32[32]{0:T(128)S(1)}, s32[32]{0:T(128)}, u32[]{:S(2)}) copy-start(s32[32]{0:T(128)} %param.21) | copy-start | bytes 388
